TPU v7x, 512 devices: a whole 4x8x8 slice. The times are simulated.
512 devices in a mesh: illum: 32 (over z_hi, y), gx: 4 (over x), gy: 4 (over z_lo, core).
Axes of the slice: x: 4, y: 8, z: 8 (z_hi: 4, z_lo: 2; z = z_hi * 2 + z_lo), core: 2. Of those that a mesh axis runs over, the one named last changes fastest.
Arguments:
- density: float32 [128, 64, 128], P('gx', 'gy'), may hold values from 0 to 1
- moment_one: float32 [128, 64, 128], P('gx', 'gy'), may hold values from -0.6 to 0.6
- moment_two: float32 [128, 64, 128], P('gx', 'gy'), may hold values from 0.0002 to 0.0006
- forward_field: bfloat16 [32, 2, 3, 128, 64, 128], P('illum', None, None, 'gx', 'gy'), may hold values from -6 to 6
- adjoint_field: bfloat16 [32, 2, 3, 128, 64, 128], P('illum', None, None, 'gx', 'gy'), may hold values from -6 to 6
- objective_weight: float32 [32], P('illum'), may hold values from 0.02 to 0.2
Outputs:
- new_density: float32 [128, 64, 128], P('gx', 'gy')
- new_moment_one: float32 [128, 64, 128], P('gx', 'gy')
- new_moment_two: float32 [128, 64, 128], P('gx', 'gy')
- physical: float32 [128, 64, 128], P('gx', 'gy')
All inputs are finite; a program needn't handle non-finite values.
Results may differ from a plain program's by a relative error of at most 0.0003.
Values sent between devices are 32-bit elements; how exact they have to be, the bound alone decides.
No kernel may reach another device: no remote copies, remote signals or barrier semaphores. Data moves between devices by JAX's collectives and lax.ppermute only.
A program may use at most 64 MiB of HBM per device.

v0:
```python
import jax
import jax.numpy as jnp
from jax import lax
from jax.sharding import PartitionSpec as P

RADIUS = 8


sharpness = 8.0
threshold = 0.5


def extended(value, sides, width):
    for axis, dim in sides:
        size, length = (lax.axis_size(axis), value.shape[dim])
        up = [(i, (i + 1) % size) for i in range(size - 1)]
        down = [(j, i) for i, j in up]
        last = lax.slice_in_dim(value, length - width, length, axis=dim)
        leading = lax.slice_in_dim(value, 0, width, axis=dim)
        before = lax.ppermute(last, axis, up)
        after = lax.ppermute(leading, axis, down)
        value = jnp.concatenate([before, value, after], axis=dim)
    return value


def split_up(value, dim, size):
    lengths = value.shape
    parts = value.reshape(*lengths[:dim], size, lengths[dim] // size, *lengths[dim + 1 :])
    return jnp.moveaxis(parts, dim, 0)


def summed_on_arrival(value, axis, dim):
    size = lax.axis_size(axis)
    parts = lax.all_to_all(split_up(value, dim, size), axis, 0, 0, tiled=True)
    return jnp.sum(parts, axis=0)


def in_order(parts, dim):
    lengths = list(parts.shape[1:])
    lengths[dim] *= parts.shape[0]
    return jnp.moveaxis(parts, 0, dim).reshape(lengths)


def from_everyone(value, axis):
    copies = jnp.broadcast_to(value, (lax.axis_size(axis), *value.shape))
    return lax.all_to_all(copies, axis, split_axis=0, concat_axis=0, tiled=True)


def gather_directly(value, axis, dim):
    return in_order(from_everyone(value, axis), dim)


def tap_weights():
    offsets = jnp.arange(-RADIUS, RADIUS + 1)
    return ((RADIUS + 1 - jnp.abs(offsets)) / (RADIUS + 1) ** 2).astype(jnp.float32)


def band_matrix(length):
    rows = jnp.arange(length)[:, None]
    cols = jnp.arange(length)[None, :]
    apart = jnp.abs(rows - cols)
    values = (RADIUS + 1 - apart).astype(jnp.float32) / float((RADIUS + 1) ** 2)
    return jnp.where(apart <= RADIUS, values, jnp.float32(0.0))


def line_filter(padded, axis, length):
    weights = tap_weights()
    total = jnp.zeros(padded.shape[:axis] + (length,) + padded.shape[axis + 1 :], jnp.float32)
    for offset in range(2 * RADIUS + 1):
        total = total + weights[offset] * lax.slice_in_dim(
            padded, offset, offset + length, axis=axis
        )
    return total


def depth_filter(field):
    shape = field.shape
    flat = field.reshape(-1, shape[2])
    out = jnp.dot(
        flat,
        band_matrix(shape[2]),
        precision=lax.Precision.HIGHEST,
        preferred_element_type=jnp.float32,
    )
    return out.reshape(shape)


def tile_filter(field):
    padded_x = extended(field, (("gx", 0),), RADIUS)
    along_x = line_filter(padded_x, 0, field.shape[0])
    padded_y = extended(along_x, (("gy", 1),), RADIUS)
    along_y = line_filter(padded_y, 1, field.shape[1])
    return depth_filter(along_y)


def project(value):
    scale = jnp.tanh(sharpness * threshold) + jnp.tanh(sharpness * (1.0 - threshold))
    return (jnp.tanh(sharpness * threshold) + jnp.tanh(sharpness * (value - threshold))) / scale


def slope(value):
    scale = jnp.tanh(sharpness * threshold) + jnp.tanh(sharpness * (1.0 - threshold))
    inner = jnp.tanh(sharpness * (value - threshold))
    return sharpness * (1.0 - inner * inner) / scale


def shards(density, moment_one, moment_two, forward_field, adjoint_field, objective_weight):
    filtered = tile_filter(density)
    real_part = forward_field[:, 0].astype(jnp.float32) * adjoint_field[:, 0].astype(jnp.float32)
    imag_part = forward_field[:, 1].astype(jnp.float32) * adjoint_field[:, 1].astype(jnp.float32)
    intersection = jnp.sum(real_part - imag_part, axis=1)
    local_term = jnp.einsum("s,sxyz->xyz", objective_weight, intersection)
    share = summed_on_arrival(local_term, "illum", 2)
    width = share.shape[2]
    offset = lax.axis_index("illum") * width
    filtered_slab = lax.dynamic_slice_in_dim(filtered, offset, width, 2)
    chained_slab = share * slope(filtered_slab)
    chained = gather_directly(chained_slab, "illum", 2)
    gradient = tile_filter(chained)
    new_moment_one = 0.9 * moment_one + 0.1 * gradient
    new_moment_two = 0.999 * moment_two + 0.001 * gradient * gradient
    first_fix = 1.0 - 0.9**5
    second_fix = 1.0 - 0.999**5
    step = new_moment_one / first_fix / (jnp.sqrt(new_moment_two / second_fix) + 1e-08)
    new_density = jnp.clip(density - 0.05 * step, 0.0, 1.0)
    physical = project(tile_filter(new_density))
    return (new_density, new_moment_one, new_moment_two, physical)


def solution(mesh):
    in_specs = (
        P("gx", "gy", None),
        P("gx", "gy", None),
        P("gx", "gy", None),
        P("illum", None, None, "gx", "gy", None),
        P("illum", None, None, "gx", "gy", None),
        P("illum"),
    )
    out_specs = (P("gx", "gy", None), P("gx", "gy", None), P("gx", "gy", None), P("gx", "gy", None))
    return jax.shard_map(shards, mesh=mesh, in_specs=in_specs, out_specs=out_specs, check_vma=False)
```

profile of v0, /device:TPU:1, one launch (start us, length us, event | category | flops | bytes accessed | tf_op | source)
XLA Modules:
  0.0 174.6 jit_solution(10467334334944862990)
XLA Ops:
  0.6 0.0 copy-start
  0.6 0.9 fusion.401
  1.6 3.9 %collective-permute-start = (f32[8,16,128]{2,1,0:T(8,128)S(1)}, f32[8,16,128]{2,1,0:T(8,128)S(1)}, u32[]{:S(2)}, u32[]{:S(2)}) collective-permute-start(f32[8,16,128]{2,1,0:T(8,128)S(1)} %get-tuple-element.19), channel_id=1, source_target_pairs={{0,4},{4,8},{8,12},{1,5},{5,9},{9,13},{2,6},{6,10},{10,14},{3,7},{... | collective-permute-start | bytes 196616 | tf_op jit(solution)/shard_map/ppermute | solution.py:20
  5.5 1.3 collective-permute-start.1
  7.5 1.6 subtract_reduce_fusion
  9.1 0.7 fusion.402
  9.8 0.0 collective-permute-done
  9.8 0.0 copy-done
  9.9 0.7 collective-permute-done.1
  10.5 11.1 %fusion.291 = f32[32,16,128]{2,1,0:T(8,128)S(1)} fusion(f32[40,16,128]{2,1,0:T(8,128)S(1)} %constant_dynamic-update-slice_fusion.2, f32[40,16,128]{2,1,0:T(8,128)S(1)} %get-tuple-element.17, f32[32,16,128]{2,1,0:T(8,128)S(1)} %copy-done, f32[]{:T(128)} %bitcast.19, f32[]{:T(128)} %bitcast.18, f32[]{:T(128)} %bitcast.17, f32[]{:T(128)} %bitcast.16, ...), kind=kLoop, calls=%fused_computation.397 | loop fusion | flops 2162688 | bytes 4718660 | tf_op jit(solution)/shard_map/add | solution.py:70
  21.6 6.0 %collective-permute-start.2 = (f32[32,8,128]{2,1,0:T(8,128)S(1)}, f32[32,8,128]{2,1,0:T(8,128)S(1)}, u32[]{:S(2)}, u32[]{:S(2)}) collective-permute-start(f32[32,8,128]{2,1,0:T(8,128)S(1)} %get-tuple-element.15), channel_id=1, source_target_pairs={{0,1},{1,2},{2,3},{4,5},{5,6},{6,7},{8,9},{9,10},{10,11},{12,13},{... | collective-permute-start | bytes 393224 | tf_op jit(solution)/shard_map/ppermute | solution.py:20
  27.6 2.6 %collective-permute-start.3 = (f32[32,8,128]{2,1,0:T(8,128)S(1)}, f32[32,8,128]{2,1,0:T(8,128)S(1)}, u32[]{:S(2)}, u32[]{:S(2)}) collective-permute-start(f32[32,8,128]{2,1,0:T(8,128)S(1)} %get-tuple-element.16), channel_id=1, source_target_pairs={{1,0},{2,1},{3,2},{5,4},{6,5},{7,6},{9,8},{10,9},{11,10},{13,12},{... | collective-permute-start | bytes 393224 | tf_op jit(solution)/shard_map/ppermute | solution.py:21
  30.3 0.5 copy.31
  30.8 1.2 reshape.107
  32.0 14.1 %all-to-all-start = ((f32[32,1,2048]{2,1,0:T(1,128)}), f32[32,1,2048]{2,1,0:T(1,128)S(1)}, u32[]{:S(2)}, u32[]{:S(2)}) async-start(f32[32,1,2048]{2,1,0:T(1,128)} %reshape.107), calls=%async_computation | async-start | bytes 524288 | tf_op jit(solution)/shard_map/all_to_all | solution.py:34
  46.1 0.0 collective-permute-done.2
  46.1 0.0 collective-permute-done.3
  46.1 13.2 %fusion.214 = f32[32,16,128]{1,2,0:T(8,128)S(1)} fusion(f32[32,16,128]{2,1,0:T(8,128)S(1)} %fusion.291, f32[32,8,128]{2,1,0:T(8,128)S(1)} %collective-permute-done.3, f32[32,8,128]{2,1,0:T(8,128)S(1)} %collective-permute-done.2, f32[]{:T(128)} %bitcast.19, f32[]{:T(128)} %bitcast.18, f32[]{:T(128)} %bitcast.17, f32[]{:T(128)} %bitcast.16, f32[]{:T(128)} %bitcast.15, ...), kind=kOutput, calls=%fused_computation.329 | convolution fusion | flops 103989248 | bytes 786500 | tf_op jit(solution)/shard_map/dot_general | solution.py:79
  59.3 0.1 copy.47
  59.4 0.2 all-to-all-done
  59.6 0.5 broadcast.94
  60.1 1.3 reduce.2
  61.4 0.3 reshape.108
  61.7 0.1 bitcast_reduce_fusion
  61.8 0.1 broadcast_bitcast_fusion
  61.9 0.5 reshape.109
  62.4 25.3 %all_to_all.10 = f32[32,1,2048]{2,1,0:T(1,128)S(1)} all-to-all(f32[32,1,2048]{2,1,0:T(1,128)S(1)} %reshape.109), channel_id=1, replica_groups=mesh['illum'=32,'gx'=4,'gy'=4] {'illum'}, dimensions={0} | all-to-all | bytes 524288 | tf_op jit(solution)/shard_map/all_to_all | solution.py:46
  87.7 1.3 reduce.3
  89.0 0.3 reshape.110
  89.3 0.1 bitcast_bitcast_fusion
  89.4 0.4 fusion.396
  89.8 0.4 copy.35
  90.2 0.0 copy-start.2
  90.2 0.0 copy-start.3
  90.2 0.4 copy.39
  90.6 1.3 collective-permute-start.5
  91.9 4.0 %collective-permute-start.4 = (f32[8,16,128]{2,1,0:T(8,128)S(1)}, f32[8,16,128]{2,1,0:T(8,128)S(1)}, u32[]{:S(2)}, u32[]{:S(2)}) collective-permute-start(f32[8,16,128]{2,1,0:T(8,128)S(1)} %copy.35), channel_id=1, source_target_pairs={{0,4},{4,8},{8,12},{1,5},{5,9},{9,13},{2,6},{6,10},{10,14},{3,7},{... | collective-permute-start | bytes 196616 | tf_op jit(solution)/shard_map/ppermute | solution.py:20
  95.9 0.5 copy.36
  96.4 0.0 collective-permute-done.5
  96.4 0.8 collective-permute-done.4
  97.2 11.1 %fusion.52 = f32[32,16,128]{2,1,0:T(8,128)S(1)} fusion(f32[32,16,128]{2,1,0:T(8,128)S(1)} %copy.36, f32[8,16,128]{2,1,0:T(8,128)S(1)} %collective-permute-done.5, f32[8,16,128]{2,1,0:T(8,128)S(1)} %collective-permute-done.4, f32[]{:T(128)} %bitcast.19, f32[]{:T(128)} %bitcast.18, f32[]{:T(128)} %bitcast.17, f32[]{:T(128)} %bitcast.16, f32[]{:T(128)} %bitcast.15, ...), kind=kLoop, calls=%fused_computation.195 | loop fusion | flops 3211264 | bytes 655428 | tf_op jit(solution)/shard_map/add | solution.py:70
  108.3 5.2 %collective-permute-start.6 = (f32[32,8,128]{2,1,0:T(8,128)S(1)}, f32[32,8,128]{2,1,0:T(8,128)S(1)}, u32[]{:S(2)}, u32[]{:S(2)}) collective-permute-start(f32[32,8,128]{2,1,0:T(8,128)S(1)} %get-tuple-element.13), channel_id=1, source_target_pairs={{0,1},{1,2},{2,3},{4,5},{5,6},{6,7},{8,9},{9,10},{10,11},{12,13},{... | collective-permute-start | bytes 393224 | tf_op jit(solution)/shard_map/ppermute | solution.py:20
  113.5 2.1 %collective-permute-start.7 = (f32[32,8,128]{2,1,0:T(8,128)S(1)}, f32[32,8,128]{2,1,0:T(8,128)S(1)}, u32[]{:S(2)}, u32[]{:S(2)}) collective-permute-start(f32[32,8,128]{2,1,0:T(8,128)S(1)} %get-tuple-element.14), channel_id=1, source_target_pairs={{1,0},{2,1},{3,2},{5,4},{6,5},{7,6},{9,8},{10,9},{11,10},{13,12},{... | collective-permute-start | bytes 393224 | tf_op jit(solution)/shard_map/ppermute | solution.py:21
  115.6 0.0 collective-permute-done.6
  115.6 4.2 %collective-permute-done.7 = f32[32,8,128]{2,1,0:T(8,128)S(1)} collective-permute-done((f32[32,8,128]{2,1,0:T(8,128)S(1)}, f32[32,8,128]{2,1,0:T(8,128)S(1)}, u32[]{:S(2)}, u32[]{:S(2)}) %collective-permute-start.7) | collective-permute-done | bytes 131104 | tf_op jit(solution)/shard_map/ppermute | solution.py:21
  119.8 0.0 copy-done.2
  119.8 0.0 copy-done.3
  119.8 12.7 %subtract_clamp_fusion = (f32[32,16,128]{2,1,0:T(8,128)S(1)}, f32[32,16,128]{2,1,0:T(8,128)}, f32[32,16,128]{2,1,0:T(8,128)}) fusion(f32[32,16,128]{2,1,0:T(8,128)S(1)} %copy-done, f32[32,16,128]{2,1,0:T(8,128)S(1)} %copy-done.2, f32[32,16,128]{2,1,0:T(8,128)S(1)} %copy-done.3, f32[32,16,128]{2,1,0:T(8,128)S(1)} %fusion.52, ...), kind=kOutput, calls=%fused_computation.429 | convolution fusion | flops 104906752 | bytes 2097220 | tf_op jit(solution)/shard_map/dot_general | solution.py:79
  132.5 0.0 copy-start.1
  132.5 4.0 %collective-permute-start.8 = (f32[8,16,128]{2,1,0:T(8,128)S(1)}, f32[8,16,128]{2,1,0:T(8,128)S(1)}, u32[]{:S(2)}, u32[]{:S(2)}) collective-permute-start(f32[8,16,128]{2,1,0:T(8,128)S(1)} %get-tuple-element.11), channel_id=1, source_target_pairs={{0,4},{4,8},{8,12},{1,5},{5,9},{9,13},{2,6},{6,10},{10,14},{3,7},{... | collective-permute-start | bytes 196616 | tf_op jit(solution)/shard_map/ppermute | solution.py:20
  136.5 1.3 collective-permute-start.9
  137.8 0.0 collective-permute-done.8
  137.8 3.7 %collective-permute-done.9 = f32[8,16,128]{2,1,0:T(8,128)S(1)} collective-permute-done((f32[8,16,128]{2,1,0:T(8,128)S(1)}, f32[8,16,128]{2,1,0:T(8,128)S(1)}, u32[]{:S(2)}, u32[]{:S(2)}) %collective-permute-start.9) | collective-permute-done | bytes 65568 | tf_op jit(solution)/shard_map/ppermute | solution.py:21
  141.5 11.1 %fusion.8 = f32[32,16,128]{2,1,0:T(8,128)S(1)} fusion(f32[32,16,128]{2,1,0:T(8,128)S(1)} %get-tuple-element.4, f32[8,16,128]{2,1,0:T(8,128)S(1)} %collective-permute-done.9, f32[8,16,128]{2,1,0:T(8,128)S(1)} %collective-permute-done.8, f32[]{:T(128)} %bitcast.19, f32[]{:T(128)} %bitcast.18, f32[]{:T(128)} %bitcast.17, f32[]{:T(128)} %bitcast.16, ...), kind=kLoop, calls=%fused_computation.151 | loop fusion | flops 3211264 | bytes 655428 | tf_op jit(solution)/shard_map/add | solution.py:70
  152.6 3.2 %collective-permute-start.10 = (f32[32,8,128]{2,1,0:T(8,128)S(1)}, f32[32,8,128]{2,1,0:T(8,128)S(1)}, u32[]{:S(2)}, u32[]{:S(2)}) collective-permute-start(f32[32,8,128]{2,1,0:T(8,128)S(1)} %get-tuple-element.9), channel_id=1, source_target_pairs={{0,1},{1,2},{2,3},{4,5},{5,6},{6,7},{8,9},{9,10},{10,11},{12,13},{... | collective-permute-start | bytes 393224 | tf_op jit(solution)/shard_map/ppermute | solution.py:20
  155.8 1.9 %collective-permute-start.11 = (f32[32,8,128]{2,1,0:T(8,128)S(1)}, f32[32,8,128]{2,1,0:T(8,128)S(1)}, u32[]{:S(2)}, u32[]{:S(2)}) collective-permute-start(f32[32,8,128]{2,1,0:T(8,128)S(1)} %get-tuple-element.10), channel_id=1, source_target_pairs={{1,0},{2,1},{3,2},{5,4},{6,5},{7,6},{9,8},{10,9},{11,10},{13,12},{... | collective-permute-start | bytes 393224 | tf_op jit(solution)/shard_map/ppermute | solution.py:21
  157.8 0.0 collective-permute-done.10
  157.8 4.3 %collective-permute-done.11 = f32[32,8,128]{2,1,0:T(8,128)S(1)} collective-permute-done((f32[32,8,128]{2,1,0:T(8,128)S(1)}, f32[32,8,128]{2,1,0:T(8,128)S(1)}, u32[]{:S(2)}, u32[]{:S(2)}) %collective-permute-start.11) | collective-permute-done | bytes 131104 | tf_op jit(solution)/shard_map/ppermute | solution.py:21
  162.1 12.5 %fusion.3 = f32[32,16,128]{2,1,0:T(8,128)} fusion(f32[32,16,128]{2,1,0:T(8,128)S(1)} %fusion.8, f32[32,8,128]{2,1,0:T(8,128)S(1)} %collective-permute-done.11, f32[32,8,128]{2,1,0:T(8,128)S(1)} %collective-permute-done.10, f32[]{:T(128)} %bitcast.19, f32[]{:T(128)} %bitcast.18, f32[]{:T(128)} %bitcast.17, f32[]{:T(128)} %bitcast.16, f32[]{:T(128)} %bitcast.15, ...), kind=kOutput, calls=%fused_computation.4 | convolution fusion | flops 104251392 | bytes 786500 | tf_op jit(solution)/shard_map/dot_general | solution.py:79
  174.6 0.0 copy-done.1
  (11 shorter events, 0.2 us)
Async XLA Ops:
  0.6 9.2 %copy-start = (f32[32,16,128]{2,1,0:T(8,128)S(1)}, f32[32,16,128]{2,1,0:T(8,128)}, u32[]{:S(2)}) copy-start(f32[32,16,128]{2,1,0:T(8,128)} %param.6) | copy-start | bytes 786436
  1.6 8.2 %collective-permute-start = (f32[8,16,128]{2,1,0:T(8,128)S(1)}, f32[8,16,128]{2,1,0:T(8,128)S(1)}, u32[]{:S(2)}, u32[]{:S(2)}) collective-permute-start(f32[8,16,128]{2,1,0:T(8,128)S(1)} %get-tuple-element.19), channel_id=1, source_target_pairs={{0,4},{4,8},{8,12},{1,5},{5,9},{9,13},{2,6},{6,10},{10,14},{3,7},{... | collective-permute-start | bytes 196616 | tf_op jit(solution)/shard_map/ppermute | solution.py:20
  5.5 5.0 %collective-permute-start.1 = (f32[8,16,128]{2,1,0:T(8,128)S(1)}, f32[8,16,128]{2,1,0:T(8,128)S(1)}, u32[]{:S(2)}, u32[]{:S(2)}) collective-permute-start(f32[8,16,128]{2,1,0:T(8,128)S(1)} %get-tuple-element.20), channel_id=1, source_target_pairs={{4,0},{8,4},{12,8},{5,1},{9,5},{13,9},{6,2},{10,6},{14,10},{7,3},{... | collective-permute-start | bytes 196616 | tf_op jit(solution)/shard_map/ppermute | solution.py:21
  21.6 24.5 %collective-permute-start.2 = (f32[32,8,128]{2,1,0:T(8,128)S(1)}, f32[32,8,128]{2,1,0:T(8,128)S(1)}, u32[]{:S(2)}, u32[]{:S(2)}) collective-permute-start(f32[32,8,128]{2,1,0:T(8,128)S(1)} %get-tuple-element.15), channel_id=1, source_target_pairs={{0,1},{1,2},{2,3},{4,5},{5,6},{6,7},{8,9},{9,10},{10,11},{12,13},{... | collective-permute-start | bytes 393224 | tf_op jit(solution)/shard_map/ppermute | solution.py:20
  27.6 18.5 %collective-permute-start.3 = (f32[32,8,128]{2,1,0:T(8,128)S(1)}, f32[32,8,128]{2,1,0:T(8,128)S(1)}, u32[]{:S(2)}, u32[]{:S(2)}) collective-permute-start(f32[32,8,128]{2,1,0:T(8,128)S(1)} %get-tuple-element.16), channel_id=1, source_target_pairs={{1,0},{2,1},{3,2},{5,4},{6,5},{7,6},{9,8},{10,9},{11,10},{13,12},{... | collective-permute-start | bytes 393224 | tf_op jit(solution)/shard_map/ppermute | solution.py:21
  32.0 27.6 %all-to-all-start = ((f32[32,1,2048]{2,1,0:T(1,128)}), f32[32,1,2048]{2,1,0:T(1,128)S(1)}, u32[]{:S(2)}, u32[]{:S(2)}) async-start(f32[32,1,2048]{2,1,0:T(1,128)} %reshape.107), calls=%async_computation | async-start | bytes 524288 | tf_op jit(solution)/shard_map/all_to_all | solution.py:34
  90.2 29.6 %copy-start.2 = (f32[32,16,128]{2,1,0:T(8,128)S(1)}, f32[32,16,128]{2,1,0:T(8,128)}, u32[]{:S(2)}) copy-start(f32[32,16,128]{2,1,0:T(8,128)} %param.7) | copy-start | bytes 786436
  90.2 29.6 %copy-start.3 = (f32[32,16,128]{2,1,0:T(8,128)S(1)}, f32[32,16,128]{2,1,0:T(8,128)}, u32[]{:S(2)}) copy-start(f32[32,16,128]{2,1,0:T(8,128)} %param.8) | copy-start | bytes 786436
  90.6 5.8 %collective-permute-start.5 = (f32[8,16,128]{2,1,0:T(8,128)S(1)}, f32[8,16,128]{2,1,0:T(8,128)S(1)}, u32[]{:S(2)}, u32[]{:S(2)}) collective-permute-start(f32[8,16,128]{2,1,0:T(8,128)S(1)} %copy.39), channel_id=1, source_target_pairs={{4,0},{8,4},{12,8},{5,1},{9,5},{13,9},{6,2},{10,6},{14,10},{7,3},{... | collective-permute-start | bytes 196616 | tf_op jit(solution)/shard_map/ppermute | solution.py:21
  91.9 5.3 %collective-permute-start.4 = (f32[8,16,128]{2,1,0:T(8,128)S(1)}, f32[8,16,128]{2,1,0:T(8,128)S(1)}, u32[]{:S(2)}, u32[]{:S(2)}) collective-permute-start(f32[8,16,128]{2,1,0:T(8,128)S(1)} %copy.35), channel_id=1, source_target_pairs={{0,4},{4,8},{8,12},{1,5},{5,9},{9,13},{2,6},{6,10},{10,14},{3,7},{... | collective-permute-start | bytes 196616 | tf_op jit(solution)/shard_map/ppermute | solution.py:20
  108.3 7.3 %collective-permute-start.6 = (f32[32,8,128]{2,1,0:T(8,128)S(1)}, f32[32,8,128]{2,1,0:T(8,128)S(1)}, u32[]{:S(2)}, u32[]{:S(2)}) collective-permute-start(f32[32,8,128]{2,1,0:T(8,128)S(1)} %get-tuple-element.13), channel_id=1, source_target_pairs={{0,1},{1,2},{2,3},{4,5},{5,6},{6,7},{8,9},{9,10},{10,11},{12,13},{... | collective-permute-start | bytes 393224 | tf_op jit(solution)/shard_map/ppermute | solution.py:20
  113.5 6.3 %collective-permute-start.7 = (f32[32,8,128]{2,1,0:T(8,128)S(1)}, f32[32,8,128]{2,1,0:T(8,128)S(1)}, u32[]{:S(2)}, u32[]{:S(2)}) collective-permute-start(f32[32,8,128]{2,1,0:T(8,128)S(1)} %get-tuple-element.14), channel_id=1, source_target_pairs={{1,0},{2,1},{3,2},{5,4},{6,5},{7,6},{9,8},{10,9},{11,10},{13,12},{... | collective-permute-start | bytes 393224 | tf_op jit(solution)/shard_map/ppermute | solution.py:21
  132.5 42.1 %copy-start.1 = (f32[32,16,128]{2,1,0:T(8,128)}, f32[32,16,128]{2,1,0:T(8,128)S(1)}, u32[]{:S(2)}) copy-start(f32[32,16,128]{2,1,0:T(8,128)S(1)} %get-tuple-element.4) | copy-start | bytes 786436
  132.5 5.3 %collective-permute-start.8 = (f32[8,16,128]{2,1,0:T(8,128)S(1)}, f32[8,16,128]{2,1,0:T(8,128)S(1)}, u32[]{:S(2)}, u32[]{:S(2)}) collective-permute-start(f32[8,16,128]{2,1,0:T(8,128)S(1)} %get-tuple-element.11), channel_id=1, source_target_pairs={{0,4},{4,8},{8,12},{1,5},{5,9},{9,13},{2,6},{6,10},{10,14},{3,7},{... | collective-permute-start | bytes 196616 | tf_op jit(solution)/shard_map/ppermute | solution.py:20
  136.5 5.0 %collective-permute-start.9 = (f32[8,16,128]{2,1,0:T(8,128)S(1)}, f32[8,16,128]{2,1,0:T(8,128)S(1)}, u32[]{:S(2)}, u32[]{:S(2)}) collective-permute-start(f32[8,16,128]{2,1,0:T(8,128)S(1)} %get-tuple-element.12), channel_id=1, source_target_pairs={{4,0},{8,4},{12,8},{5,1},{9,5},{13,9},{6,2},{10,6},{14,10},{7,3},{... | collective-permute-start | bytes 196616 | tf_op jit(solution)/shard_map/ppermute | solution.py:21
  152.6 5.2 %collective-permute-start.10 = (f32[32,8,128]{2,1,0:T(8,128)S(1)}, f32[32,8,128]{2,1,0:T(8,128)S(1)}, u32[]{:S(2)}, u32[]{:S(2)}) collective-permute-start(f32[32,8,128]{2,1,0:T(8,128)S(1)} %get-tuple-element.9), channel_id=1, source_target_pairs={{0,1},{1,2},{2,3},{4,5},{5,6},{6,7},{8,9},{9,10},{10,11},{12,13},{... | collective-permute-start | bytes 393224 | tf_op jit(solution)/shard_map/ppermute | solution.py:20
  155.8 6.3 %collective-permute-start.11 = (f32[32,8,128]{2,1,0:T(8,128)S(1)}, f32[32,8,128]{2,1,0:T(8,128)S(1)}, u32[]{:S(2)}, u32[]{:S(2)}) collective-permute-start(f32[32,8,128]{2,1,0:T(8,128)S(1)} %get-tuple-element.10), channel_id=1, source_target_pairs={{1,0},{2,1},{3,2},{5,4},{6,5},{7,6},{9,8},{10,9},{11,10},{13,12},{... | collective-permute-start | bytes 393224 | tf_op jit(solution)/shard_map/ppermute | solution.py:21
where the time goes:
time: 176 us; the launch traced here: 175 us
  starting transfers between devices  50.9 us (29%)
  matrix products  38.4 us (22%)
  other arithmetic  37.4 us (21%)
  blocking collectives  25.3 us (14%)
  waiting for transfers between devices  13.9 us (8%)
  local copies, waits for them, and re-layouts  7.12 us (4%)
    dot_general x3, matrix products, depth_filter(): jnp.dot(flat, band_matrix(shape[2]), precision=lax.Precision.HIGHEST, pre...  38.4 us
    add x3, other arithmetic, line_filter(): total + weights[offset] * lax.slice_in_dim(padded, offset, offset + lengt...  33.2 us
    ppermute x6, starting transfers between devices, extended(): before = lax.ppermute(last, axis, up)  26.3 us
    all_to_all x1, blocking collectives, from_everyone(): return lax.all_to_all(copies, axis, split_axis=0, concat_axis=0, tiled=True)  25.3 us
    all_to_all x1, starting transfers between devices, summed_on_arrival(): parts = lax.all_to_all(split_up(value, dim, size), axis, 0, 0, tiled=True)  14.1 us
    ppermute x6, waiting for transfers between devices, extended(): after = lax.ppermute(leading, axis, down)  12.9 us
    ppermute x6, starting transfers between devices, extended(): after = lax.ppermute(leading, axis, down)  10.5 us
  transfers between devices with their start and end apart: 13, of which 6 were waited for; matrix products, arithmetic and copies ran while one was open for 10% of the time, Pallas kernels for 0%

commit v1 on v0

v1 whole, which is shorter than its diff:
```python
import functools

import jax
import jax.numpy as jnp
import numpy as np
from jax import lax
from jax.experimental import pallas as pl
from jax.experimental.pallas import tpu as pltpu
from jax.sharding import PartitionSpec as P

RADIUS = 8
TAPS = RADIUS + 1
UNIT = 1.0 / float(TAPS**2)
sharpness = 8.0
threshold = 0.5

GROUPS = 4
SLABS = 32
DEEP = 4


def call(kernel, out_shape, **more):
    return pl.pallas_call(
        kernel,
        out_shape=out_shape,
        compiler_params=pltpu.CompilerParams(vmem_limit_bytes=48 * 1024 * 1024),
        **more,
    )


def whole(count):
    return [pl.BlockSpec(memory_space=pltpu.VMEM)] * count


def hat(a, b):
    return jnp.maximum(TAPS - jnp.abs(a - b), 0)


def bf(value):
    return value.astype(jnp.bfloat16)


def f32(value):
    return value.astype(jnp.float32)


def parts_of(value, count):
    out = []
    for _ in range(count):
        part = bf(value)
        out.append(part)
        value = value - f32(part)
    return out


def dot(a, b, dims):
    return lax.dot_general(a, b, (dims, ((), ())), preferred_element_type=jnp.float32)


def iota(shape, dim):
    return lax.broadcasted_iota(jnp.int32, shape, dim)


def sensitivity_kernel(fwd_ref, adj_ref, weight_ref, density_ref, terms_ref, own_ref):
    slab = lax.axis_index("illum")
    total = None
    for component in range(3):
        real = f32(fwd_ref[0, 0, component]) * f32(adj_ref[0, 0, component])
        imag = f32(fwd_ref[0, 1, component]) * f32(adj_ref[0, 1, component])
        term = real - imag
        total = term if total is None else total + term
    total = (total * weight_ref[0]).reshape(256, 128)
    side = jnp.concatenate([total[:128], total[128:]], axis=1)
    rows, cols = iota((256, 256), 0), iota((256, 256), 1)
    group = ((rows >> 2) & 1) == (cols >> 7)
    depth = (rows >> 3) * DEEP + (rows & 3)
    pick = bf(jnp.where(group & (depth == (cols & 127)), 1.0, 0.0))
    turned = sum(dot(pick, part, ((1,), (1,))) for part in parts_of(side, 3))
    terms_ref[...] = turned.reshape(32, 8, 128)
    dens = density_ref[...].reshape(256, 128)
    dens = jnp.concatenate([dens[:128], dens[128:]], axis=1)
    rows, cols = iota((8, 256), 0), iota((8, 256), 1)
    near = hat(slab * DEEP + (rows & 3), cols & 127)
    band = bf(jnp.where(((rows >> 2) & 1) == (cols >> 7), near, 0).astype(jnp.float32))
    own_ref[...] = sum(dot(band, part, ((1,), (1,))) for part in parts_of(dens, 3))


def sensitivity(fwd, adj, weight, density):
    return call(
        sensitivity_kernel,
        (jax.ShapeDtypeStruct((SLABS, 16, 128), jnp.float32), jax.ShapeDtypeStruct((16, 128), jnp.float32)),
        grid=(2,),
        in_specs=[
            pl.BlockSpec((1, 2, 3, 16, 16, 128), lambda i: (0, 0, 0, i, 0, 0)),
            pl.BlockSpec((1, 2, 3, 16, 16, 128), lambda i: (0, 0, 0, i, 0, 0)),
            pl.BlockSpec(memory_space=pltpu.SMEM),
            pl.BlockSpec((16, 16, 128), lambda i: (i, 0, 0)),
        ],
        out_specs=(
            pl.BlockSpec((SLABS, 8, 128), lambda i: (0, i, 0)),
            pl.BlockSpec((8, 128), lambda i: (i, 0)),
        ),
    )(fwd, adj, weight, density)


def sum_kernel(terms_ref, own_ref, out_ref):
    both = jnp.concatenate([jnp.sum(terms_ref[...], axis=0), own_ref[...]], axis=0)
    out_ref[...] = jnp.broadcast_to(both[None], out_ref.shape)


def summed(terms, own):
    return call(
        sum_kernel,
        jax.ShapeDtypeStruct((16, 32, 128), jnp.float32),
        in_specs=whole(2),
        out_specs=whole(1)[0],
    )(terms, own)


def plane_taps():
    dx, dy, x, y = np.meshgrid(np.arange(-1, 2), np.arange(-1, 2), np.arange(8), np.arange(16), indexing="ij")
    far_x = (x + 8 * dx).reshape(-1, 1) - np.repeat(np.arange(8), 16)
    far_y = (y + 16 * dy).reshape(-1, 1) - np.tile(np.arange(16), 8)
    taps = np.maximum(TAPS - np.abs(far_x), 0) * np.maximum(TAPS - np.abs(far_y), 0)
    return jnp.asarray(taps.astype(np.float32)).astype(jnp.bfloat16)


PAD_X, PAD_Y = 3, 2


def slab_kernel(all_ref, taps_ref, out_ref, sens, dens):
    gx, gy = lax.axis_index("gx"), lax.axis_index("gy")
    low = iota((8, 128), 0) < DEEP
    zero = jnp.zeros((8, 128), jnp.float32)
    for ref in (sens, dens):
        for x in range(16 + 2 * PAD_X):
            for y in range(4 + 2 * PAD_Y):
                if not (PAD_X <= x < 16 + PAD_X and PAD_Y <= y < 4 + PAD_Y):
                    ref[x, y] = zero
    for x in range(4):
        for y in range(4):
            for pair in range(2):
                at = PAD_X + 4 * x + 2 * pair
                for ref, base in ((sens, 0), (dens, 16)):
                    tile = all_ref[4 * x + y, base + 8 * pair : base + 8 * pair + 8, :]
                    turned = pltpu.roll(tile, DEEP, 0)
                    twice = (jnp.where(low, tile, turned), jnp.where(low, turned, tile))
                    for odd in range(2):
                        value = twice[odd]
                        if base:
                            top = f32(bf(value))
                            value = jnp.where(low, top, value - top)
                        ref[at + odd, PAD_Y + y] = value
    taps = taps_ref[...]
    first = GROUPS * gx
    window = dens[pl.ds(first, 10), pl.ds(gy, 5)]
    side = jnp.concatenate(
        [bf(window[dx : dx + 8, dy : dy + 3].reshape(192, 128)) for dx in range(3) for dy in range(3)], axis=1
    )
    filtered = dot(side, taps, ((1,), (0,))).reshape(24, 8, 128)
    filtered = (filtered + pltpu.roll(filtered, DEEP, 1)) * (UNIT * UNIT * UNIT)
    inner = jnp.tanh(sharpness * (filtered - threshold))
    scale = jnp.tanh(jnp.full((8, 128), sharpness * threshold, jnp.float32)) * 2.0
    slope = sharpness * (1.0 - inner * inner) / scale
    chained = slope * sens[pl.ds(first + 1, 8), pl.ds(gy + 1, 3)].reshape(24, 8, 128)
    top = f32(bf(chained))
    chained = bf(jnp.where(low, top, chained - top)).reshape(8, 3, 8, 128)
    side = jnp.concatenate([chained[dx : dx + 6, dy].reshape(48, 128) for dx in range(3) for dy in range(3)], axis=1)
    result = dot(side, taps, ((1,), (0,))).reshape(6, 8, 128)
    result = result + pltpu.roll(result, DEEP, 1)
    for pair in range(3):
        tile = jnp.where(low, result[2 * pair], result[2 * pair + 1])
        out_ref[:, 8 * pair : 8 * pair + 8, :] = jnp.broadcast_to(tile[None], (SLABS, 8, 128))


def slab_step(everything):
    return call(
        slab_kernel,
        jax.ShapeDtypeStruct((SLABS, 24, 128), jnp.float32),
        in_specs=whole(2),
        out_specs=whole(1)[0],
        scratch_shapes=[pltpu.VMEM((16 + 2 * PAD_X, 4 + 2 * PAD_Y, 8, 128), jnp.float32)] * 2,
    )(everything, plane_taps())


def adam(density, moment_one, moment_two, gradient):
    new_one = 0.9 * moment_one + 0.1 * gradient
    new_two = 0.999 * moment_two + 0.001 * gradient * gradient
    first_fix = 1.0 - 0.9**5
    second_fix = 1.0 - 0.999**5
    step = new_one / first_fix / (jnp.sqrt(new_two / second_fix) + 1e-08)
    return jnp.clip(density - 0.05 * step, 0.0, 1.0), new_one, new_two


def box(value):
    n = value.shape[0]
    two = value[: n - 1] + value[1:]
    four = two[: n - 3] + two[2:]
    eight = four[: n - 7] + four[4:]
    return eight[: n - 8] + value[8:]


def adam_kernel(slabs_ref, d_ref, m_ref, v_ref, left_ref, right_ref, nd_ref, nm_ref, nv_ref, fx_ref, lo_ref, hi_ref, ext):
    gx = lax.axis_index("gx")
    rows, cols = iota((256, 256), 0), iota((256, 256), 1)
    depth = (rows >> 3) * DEEP + (rows & 3)
    near = jnp.where(((rows >> 2) & 1) == (cols >> 7), hat(depth, cols & 127), 0)
    band = bf(near.astype(jnp.float32))
    for pair in range(3):
        side = slabs_ref[:, 8 * pair : 8 * pair + 8, :].reshape(256, 128)
        both = sum(dot(part, band, ((0,), (0,))) for part in parts_of(side, 2)) * (UNIT * UNIT * UNIT)
        for odd in range(2):
            group = 2 * pair + odd - 1
            gradient = both[:, 128 * odd : 128 * odd + 128].reshape(8, 16, 128)
            if group == -1:
                new, _, _ = adam(left_ref[0], left_ref[1], left_ref[2], gradient)
                new = jnp.where(gx > 0, new, 0.0)
            elif group == GROUPS:
                new, _, _ = adam(right_ref[0], right_ref[1], right_ref[2], gradient)
                new = jnp.where(gx < lax.axis_size("gx") - 1, new, 0.0)
            else:
                at = slice(8 * group, 8 * group + 8)
                new, one, two = adam(d_ref[at], m_ref[at], v_ref[at], gradient)
                nd_ref[at] = new
                nm_ref[at] = one
                nv_ref[at] = two
            ext[8 * (group + 1) : 8 * (group + 1) + 8] = new
    along_x = box(box(ext[...])) * UNIT
    fx_ref[...] = along_x
    lo_ref[...] = along_x[:, :8]
    hi_ref[...] = along_x[:, 8:]


def adam_step(slabs, density, moment_one, moment_two, left, right):
    tile = jax.ShapeDtypeStruct((32, 16, 128), jnp.float32)
    half = jax.ShapeDtypeStruct((32, 8, 128), jnp.float32)
    return call(
        adam_kernel,
        (tile, tile, tile, tile, half, half),
        in_specs=whole(6),
        out_specs=tuple(whole(6)),
        scratch_shapes=[pltpu.VMEM((48, 16, 128), jnp.float32)],
    )(slabs, density, moment_one, moment_two, left, right)


def physical_kernel(fx_ref, before_ref, after_ref, out_ref):
    rows, cols = iota((128, 256), 0), iota((128, 256), 1)
    own = cols - 64
    late = cols - 192
    before, after = cols < 64, cols >= 192
    x = jnp.where(before, cols >> 3, jnp.where(after, late >> 3, own >> 4))
    y = jnp.where(before, (cols & 7) - 8, jnp.where(after, (late & 7) + 16, own & 15))
    spread = bf(jnp.where(x == (rows >> 4), hat(y, rows & 15), 0).astype(jnp.float32))
    band = bf(hat(iota((128, 128), 0), iota((128, 128), 1)).astype(jnp.float32))
    scale = jnp.tanh(jnp.full((128, 128), sharpness * threshold, jnp.float32))
    for pair in range(2):
        sides = []
        for odd in range(2):
            at = slice(8 * (2 * pair + odd), 8 * (2 * pair + odd) + 8)
            sides.append(
                jnp.concatenate(
                    [
                        before_ref[at].reshape(64, 128),
                        fx_ref[at].reshape(128, 128),
                        after_ref[at].reshape(64, 128),
                    ],
                    axis=0,
                )
            )
        side = jnp.concatenate(sides, axis=1)
        both = sum(dot(spread, part, ((1,), (0,))) for part in parts_of(side, 2))
        for odd in range(2):
            at = slice(8 * (2 * pair + odd), 8 * (2 * pair + odd) + 8)
            along_y = both[:, 128 * odd : 128 * odd + 128]
            value = sum(dot(part, band, ((1,), (0,))) for part in parts_of(along_y, 2)) * (UNIT * UNIT)
            value = (scale + jnp.tanh(sharpness * (value - threshold))) / (scale + scale)
            out_ref[at] = value.reshape(8, 16, 128)


def physical_step(along_x, before, after):
    return call(
        physical_kernel,
        jax.ShapeDtypeStruct((32, 16, 128), jnp.float32),
        in_specs=whole(3),
        out_specs=whole(1)[0],
    )(along_x, before, after)


def neighbours(last, leading, axis):
    size = lax.axis_size(axis)
    up = [(i, i + 1) for i in range(size - 1)]
    down = [(j, i) for i, j in up]
    return lax.ppermute(last, axis, up), lax.ppermute(leading, axis, down)


def exchange(value, axes):
    return lax.all_to_all(value, axes, 0, 0, tiled=True)


def shards(density, moment_one, moment_two, forward_field, adjoint_field, objective_weight):
    stacked = jnp.stack([density, moment_one, moment_two])
    left, right = neighbours(stacked[:, 24:], stacked[:, :8], "gx")
    terms, own = sensitivity(forward_field, adjoint_field, objective_weight, density)
    terms = exchange(terms, "illum")
    everything = exchange(summed(terms, own), ("gx", "gy"))
    slabs = exchange(slab_step(everything), "illum")
    new_density, new_one, new_two, along_x, leading, last = adam_step(
        slabs, density, moment_one, moment_two, left, right
    )
    before, after = neighbours(last, leading, "gy")
    physical = physical_step(along_x, before, after)
    return (new_density, new_one, new_two, physical)


def solution(mesh):
    tile = P("gx", "gy", None)
    field = P("illum", None, None, "gx", "gy", None)
    return jax.shard_map(
        shards,
        mesh=mesh,
        in_specs=(tile, tile, tile, field, field, P("illum")),
        out_specs=(tile, tile, tile, tile),
        check_vma=False,
    )
```

time: 176 us -> 85.4 us (0.49)
  matrix products: 38.4 us -> 0 us
  other arithmetic: 37.4 us -> 0.03 us
  starting transfers between devices: 50.9 us -> 16.8 us
  blocking collectives: 25.3 us -> 44.5 us
  Pallas kernels: 0 us -> 5.14 us
  local copies, waits for them, and re-layouts: 7.12 us -> 3.23 us
    dot_general x3 -> x0, matrix products: 38.4 us -> none  [depth_filter(): jnp.dot(flat, band_matrix(shape[2]), precision=lax.Precision.HIGHEST, pre...]
    add x3 -> x0, other arithmetic: 33.2 us -> none  [line_filter(): total + weights[offset] * lax.slice_in_dim(padded, offset, offset + lengt...]
    ppermute x12 -> x4, starting transfers between devices: 36.8 us -> 12.8 us  [neighbours(): return (lax.ppermute(last, axis, up), lax.ppermute(leading, axis, down))]
    all_to_all x1 -> x2, blocking collectives: 25.3 us -> 44.5 us  [exchange(): return lax.all_to_all(value, axes, 0, 0, tiled=True)]
    all_to_all x1, starting transfers between devices: 14.1 us -> 4.01 us  [exchange(): return lax.all_to_all(value, axes, 0, 0, tiled=True)]
    ppermute x12 -> x4, waiting for transfers between devices: 13.7 us -> 7.25 us  [neighbours(): return (lax.ppermute(last, axis, up), lax.ppermute(leading, axis, down))]
    all_to_all x1, waiting for transfers between devices: 0.17 us -> 6.36 us  [exchange(): return lax.all_to_all(value, axes, 0, 0, tiled=True)]
    pallas_call x0 -> x5, Pallas kernels: none -> 5.14 us  [the longest x1 1.58 us: adam_step(): call(adam_kernel, (tile, tile, tile, tile, half, half), in_specs=whole(6)...]
  transfers between devices with their start and end apart: 13 -> 5, of which waited for: 6 -> 4; matrix products, arithmetic and copies ran while one was open for 10% -> 0% of each run, Pallas kernels for 0% -> 0%
where the time goes in v1:
time: 85.4 us; the launch traced here: 84.7 us
  blocking collectives  44.5 us (52%)
  starting transfers between devices  16.8 us (20%)
  waiting for transfers between devices  13.6 us (16%)
  Pallas kernels  5.14 us (6%)
  local copies, waits for them, and re-layouts  3.23 us (4%)
  between operations  1.4 us (2%)
    all_to_all x2, blocking collectives, exchange(): return lax.all_to_all(value, axes, 0, 0, tiled=True)  44.5 us
    ppermute x4, starting transfers between devices, neighbours(): return (lax.ppermute(last, axis, up), lax.ppermute(leading, axis, down))  12.8 us
    ppermute x4, waiting for transfers between devices, neighbours(): return (lax.ppermute(last, axis, up), lax.ppermute(leading, axis, down))  7.25 us
    all_to_all x1, waiting for transfers between devices, exchange(): return lax.all_to_all(value, axes, 0, 0, tiled=True)  6.36 us
    all_to_all x1, starting transfers between devices, exchange(): return lax.all_to_all(value, axes, 0, 0, tiled=True)  4.01 us
    unnamed x14, local copies, waits for them, and re-layouts  3.23 us
  transfers between devices with their start and end apart: 5, of which 4 were waited for; matrix products, arithmetic and copies ran while one was open for 0% of the time, Pallas kernels for 0%

profile of v1, /device:TPU:1, one launch (start us, length us, event | category | flops | bytes accessed | tf_op | source)
XLA Modules:
  0.0 84.7 jit_solution(1365139565052532489)
XLA Ops:
  1.3 0.0 copy-start
  1.3 0.9 %copy-done = f32[32,16,128]{2,1,0:T(8,128)S(1)} copy-done((f32[32,16,128]{2,1,0:T(8,128)S(1)}, f32[32,16,128]{2,1,0:T(8,128)}, u32[]{:S(2)}) %copy-start) | copy-done | bytes 262168
  2.2 0.0 copy-start.4
  2.2 1.1 %copy-done.4 = bf16[1,2,3,32,16,128]{5,4,3,2,1,0:T(8,128)(2,1)S(1)} copy-done((bf16[1,2,3,32,16,128]{5,4,3,2,1,0:T(8,128)(2,1)S(1)}, bf16[1,2,3,32,16,128]{5,4,3,2,1,0:T(8,128)(2,1)}, u32[]{:S(2)}) %copy-start.4) | copy-done | bytes 786456
  3.4 0.0 copy-start.5
  3.4 1.1 %copy-done.5 = bf16[1,2,3,32,16,128]{5,4,3,2,1,0:T(8,128)(2,1)S(1)} copy-done((bf16[1,2,3,32,16,128]{5,4,3,2,1,0:T(8,128)(2,1)S(1)}, bf16[1,2,3,32,16,128]{5,4,3,2,1,0:T(8,128)(2,1)}, u32[]{:S(2)}) %copy-start.5) | copy-done | bytes 786456
  4.5 1.0 %shard_map.102 = (f32[32,16,128]{2,1,0:T(8,128)S(1)}, f32[16,128]{1,0:T(8,128)S(1)}) custom-call(bf16[1,2,3,32,16,128]{5,4,3,2,1,0:T(8,128)(2,1)S(1)} %copy-done.4, bf16[1,2,3,32,16,128]{5,4,3,2,1,0:T(8,128)(2,1)S(1)} %copy-done.5, f32[1]{0:T(128)S(6)} %copy.11.weight_ref, f32[32,16,128]{2,1,0:T(8,128)S(1)} %copy-done), custom_call_target="tpu_custom_call" | custom-call | tf_op jit(solution)/shard_map/pallas_call | solution.py:89
  5.5 28.9 %all_to_all.15.terms_ref = f32[32,16,128]{2,1,0:T(8,128)S(1)} all-to-all(f32[32,16,128]{2,1,0:T(8,128)S(1)} %get-tuple-element.12), channel_id=1, replica_groups=mesh['illum'=32,'gx'=4,'gy'=4] {'illum'}, dimensions={0} | all-to-all | bytes 524288 | tf_op jit(solution)/shard_map/all_to_all | solution.py:297
  34.5 0.0 copy-start.6
  34.5 15.5 %all_to_all.16.all_ref = f32[16,32,128]{2,1,0:T(8,128)S(1)} all-to-all(f32[16,32,128]{2,1,0:T(8,128)S(1)} %shard_map.103), channel_id=1, replica_groups=mesh['illum'=32,'gx'=4,'gy'=4] {'gx','gy'}, dimensions={0} | all-to-all | bytes 524288 | tf_op jit(solution)/shard_map/all_to_all | solution.py:297
  50.1 0.0 copy-done.6
  50.1 1.3 %shard_map.104 = f32[32,24,128]{2,1,0:T(8,128)} custom-call(f32[16,32,128]{2,1,0:T(8,128)S(1)} %all_to_all.16.all_ref, bf16[1152,128]{1,0:T(8,128)(2,1)S(1)} %copy-done.6), custom_call_target="tpu_custom_call" | custom-call | tf_op jit(solution)/shard_map/pallas_call | solution.py:177
  51.4 0.0 copy-start.1
  51.4 0.0 copy-start.2
  51.4 0.0 copy-start.3
  51.4 4.0 %all-to-all-start.2 = ((f32[32,24,128]{2,1,0:T(8,128)}), f32[32,24,128]{2,1,0:T(8,128)S(1)}, u32[]{:S(2)}, u32[]{:S(2)}) async-start(f32[32,24,128]{2,1,0:T(8,128)} %shard_map.104), calls=%async_computation.2 | async-start | bytes 786432 | tf_op jit(solution)/shard_map/all_to_all | solution.py:297
  55.4 0.0 copy-done.1
  55.4 0.0 copy-done.2
  55.4 0.0 copy-done.3
  55.5 1.3 %collective-permute-start.1 = (f32[3,8,16,128]{3,2,1,0:T(8,128)S(1)}, f32[3,8,16,128]{3,2,1,0:T(8,128)S(1)}, u32[]{:S(2)}, u32[]{:S(2)}) collective-permute-start(f32[3,8,16,128]{3,2,1,0:T(8,128)S(1)} %get-tuple-element.20), channel_id=1, source_target_pairs={{4,0},{8,4},{12,8},{5,1},{9,5},{13,9},{6,2},{10,6},{14,10},{7,3},{... | collective-permute-start | bytes 589832 | tf_op jit(solution)/shard_map/ppermute | solution.py:293
  56.8 4.0 %collective-permute-start = (f32[3,8,16,128]{3,2,1,0:T(8,128)S(1)}, f32[3,8,16,128]{3,2,1,0:T(8,128)S(1)}, u32[]{:S(2)}, u32[]{:S(2)}) collective-permute-start(f32[3,8,16,128]{3,2,1,0:T(8,128)S(1)} %get-tuple-element.21), channel_id=1, source_target_pairs={{0,4},{4,8},{8,12},{1,5},{5,9},{9,13},{2,6},{6,10},{10,14},{3,7},{... | collective-permute-start | bytes 589832 | tf_op jit(solution)/shard_map/ppermute | solution.py:293
  60.8 2.0 %collective-permute-done.1.right_ref = f32[3,8,16,128]{3,2,1,0:T(8,128)S(1)} collective-permute-done((f32[3,8,16,128]{3,2,1,0:T(8,128)S(1)}, f32[3,8,16,128]{3,2,1,0:T(8,128)S(1)}, u32[]{:S(2)}, u32[]{:S(2)}) %collective-permute-start.1) | collective-permute-done | bytes 196640 | tf_op jit(solution)/shard_map/ppermute | solution.py:293
  62.8 0.9 %collective-permute-done.left_ref = f32[3,8,16,128]{3,2,1,0:T(8,128)S(1)} collective-permute-done((f32[3,8,16,128]{3,2,1,0:T(8,128)S(1)}, f32[3,8,16,128]{3,2,1,0:T(8,128)S(1)}, u32[]{:S(2)}, u32[]{:S(2)}) %collective-permute-start) | collective-permute-done | bytes 196640 | tf_op jit(solution)/shard_map/ppermute | solution.py:293
  63.7 6.4 %all-to-all-done.2.slabs_ref = f32[32,24,128]{2,1,0:T(8,128)S(1)} async-done(((f32[32,24,128]{2,1,0:T(8,128)}), f32[32,24,128]{2,1,0:T(8,128)S(1)}, u32[]{:S(2)}, u32[]{:S(2)}) %all-to-all-start.2) | async-done | bytes 393248 | tf_op jit(solution)/shard_map/all_to_all | solution.py:297
  70.0 1.6 %shard_map.105 = (f32[32,16,128]{2,1,0:T(8,128)}, f32[32,16,128]{2,1,0:T(8,128)}, f32[32,16,128]{2,1,0:T(8,128)}, f32[32,16,128]{2,1,0:T(8,128)S(1)}, f32[32,8,1...) custom-call(f32[32,24,128]{2,1,0:T(8,128)S(1)} %all-to-all-done.2.slabs_ref, f32[32,16,128]{2,1,0:T(8,128)S(1)} %copy-done.1, ...), custom_call_target="tpu_custom_call" | custom-call | tf_op jit(solution)/shard_map/pallas_call | solution.py:237
  71.6 5.6 %collective-permute-start.2 = (f32[32,8,128]{2,1,0:T(8,128)S(1)}, f32[32,8,128]{2,1,0:T(8,128)S(1)}, u32[]{:S(2)}, u32[]{:S(2)}) collective-permute-start(f32[32,8,128]{2,1,0:T(8,128)S(1)} %get-tuple-element.18), channel_id=1, source_target_pairs={{0,1},{1,2},{2,3},{4,5},{5,6},{6,7},{8,9},{9,10},{10,11},{12,13},{... | collective-permute-start | bytes 393224 | tf_op jit(solution)/shard_map/ppermute | solution.py:293
  77.2 1.9 %collective-permute-start.3 = (f32[32,8,128]{2,1,0:T(8,128)S(1)}, f32[32,8,128]{2,1,0:T(8,128)S(1)}, u32[]{:S(2)}, u32[]{:S(2)}) collective-permute-start(f32[32,8,128]{2,1,0:T(8,128)S(1)} %get-tuple-element.19), channel_id=1, source_target_pairs={{1,0},{2,1},{3,2},{5,4},{6,5},{7,6},{9,8},{10,9},{11,10},{13,12},{... | collective-permute-start | bytes 393224 | tf_op jit(solution)/shard_map/ppermute | solution.py:293
  79.1 0.0 collective-permute-done.2.before_ref
  79.1 4.3 %collective-permute-done.3.after_ref = f32[32,8,128]{2,1,0:T(8,128)S(1)} collective-permute-done((f32[32,8,128]{2,1,0:T(8,128)S(1)}, f32[32,8,128]{2,1,0:T(8,128)S(1)}, u32[]{:S(2)}, u32[]{:S(2)}) %collective-permute-start.3) | collective-permute-done | bytes 131104 | tf_op jit(solution)/shard_map/ppermute | solution.py:293
  83.5 1.2 %shard_map.106 = f32[32,16,128]{2,1,0:T(8,128)} custom-call(f32[32,16,128]{2,1,0:T(8,128)S(1)} %get-tuple-element.17.fx_ref, f32[32,8,128]{2,1,0:T(8,128)S(1)} %collective-permute-done.2.before_ref, f32[32,8,128]{2,1,0:T(8,128)S(1)} %collective-permute-done.3.after_ref), custom_call_target="tpu_custom_call" | custom-call | tf_op jit(solution)/shard_map/pallas_call | solution.py:281
  (2 shorter events, 0.1 us)
Async XLA Ops:
  1.3 1.0 %copy-start = (f32[32,16,128]{2,1,0:T(8,128)S(1)}, f32[32,16,128]{2,1,0:T(8,128)}, u32[]{:S(2)}) copy-start(f32[32,16,128]{2,1,0:T(8,128)} %d_ref.1) | copy-start | bytes 786436
  2.2 1.1 %copy-start.4 = (bf16[1,2,3,32,16,128]{5,4,3,2,1,0:T(8,128)(2,1)S(1)}, bf16[1,2,3,32,16,128]{5,4,3,2,1,0:T(8,128)(2,1)}, u32[]{:S(2)}) copy-start(bf16[1,2,3,32,16,128]{5,4,3,2,1,0:T(8,128)(2,1)} %fwd_ref.1) | copy-start | bytes 2359300
  3.4 1.1 %copy-start.5 = (bf16[1,2,3,32,16,128]{5,4,3,2,1,0:T(8,128)(2,1)S(1)}, bf16[1,2,3,32,16,128]{5,4,3,2,1,0:T(8,128)(2,1)}, u32[]{:S(2)}) copy-start(bf16[1,2,3,32,16,128]{5,4,3,2,1,0:T(8,128)(2,1)} %adj_ref.1) | copy-start | bytes 2359300
  34.5 15.5 %copy-start.6 = (bf16[1152,128]{1,0:T(8,128)(2,1)S(1)}, bf16[1152,128]{1,0:T(8,128)(2,1)}, u32[]{:S(2)}) copy-start(bf16[1152,128]{1,0:T(8,128)(2,1)} %constant.6.taps_ref) | copy-start | bytes 884740
  51.4 4.0 %copy-start.1 = (f32[32,16,128]{2,1,0:T(8,128)S(1)}, f32[32,16,128]{2,1,0:T(8,128)}, u32[]{:S(2)}) copy-start(f32[32,16,128]{2,1,0:T(8,128)} %d_ref.1) | copy-start | bytes 786436
  51.4 4.0 %copy-start.2 = (f32[32,16,128]{2,1,0:T(8,128)S(1)}, f32[32,16,128]{2,1,0:T(8,128)}, u32[]{:S(2)}) copy-start(f32[32,16,128]{2,1,0:T(8,128)} %m_ref.1) | copy-start | bytes 786436
  51.4 4.0 %copy-start.3 = (f32[32,16,128]{2,1,0:T(8,128)S(1)}, f32[32,16,128]{2,1,0:T(8,128)}, u32[]{:S(2)}) copy-start(f32[32,16,128]{2,1,0:T(8,128)} %v_ref.1) | copy-start | bytes 786436
  51.4 18.7 %all-to-all-start.2 = ((f32[32,24,128]{2,1,0:T(8,128)}), f32[32,24,128]{2,1,0:T(8,128)S(1)}, u32[]{:S(2)}, u32[]{:S(2)}) async-start(f32[32,24,128]{2,1,0:T(8,128)} %shard_map.104), calls=%async_computation.2 | async-start | bytes 786432 | tf_op jit(solution)/shard_map/all_to_all | solution.py:297
  55.5 7.3 %collective-permute-start.1 = (f32[3,8,16,128]{3,2,1,0:T(8,128)S(1)}, f32[3,8,16,128]{3,2,1,0:T(8,128)S(1)}, u32[]{:S(2)}, u32[]{:S(2)}) collective-permute-start(f32[3,8,16,128]{3,2,1,0:T(8,128)S(1)} %get-tuple-element.20), channel_id=1, source_target_pairs={{4,0},{8,4},{12,8},{5,1},{9,5},{13,9},{6,2},{10,6},{14,10},{7,3},{... | collective-permute-start | bytes 589832 | tf_op jit(solution)/shard_map/ppermute | solution.py:293
  56.8 6.9 %collective-permute-start = (f32[3,8,16,128]{3,2,1,0:T(8,128)S(1)}, f32[3,8,16,128]{3,2,1,0:T(8,128)S(1)}, u32[]{:S(2)}, u32[]{:S(2)}) collective-permute-start(f32[3,8,16,128]{3,2,1,0:T(8,128)S(1)} %get-tuple-element.21), channel_id=1, source_target_pairs={{0,4},{4,8},{8,12},{1,5},{5,9},{9,13},{2,6},{6,10},{10,14},{3,7},{... | collective-permute-start | bytes 589832 | tf_op jit(solution)/shard_map/ppermute | solution.py:293
  71.6 7.5 %collective-permute-start.2 = (f32[32,8,128]{2,1,0:T(8,128)S(1)}, f32[32,8,128]{2,1,0:T(8,128)S(1)}, u32[]{:S(2)}, u32[]{:S(2)}) collective-permute-start(f32[32,8,128]{2,1,0:T(8,128)S(1)} %get-tuple-element.18), channel_id=1, source_target_pairs={{0,1},{1,2},{2,3},{4,5},{5,6},{6,7},{8,9},{9,10},{10,11},{12,13},{... | collective-permute-start | bytes 393224 | tf_op jit(solution)/shard_map/ppermute | solution.py:293
  77.2 6.3 %collective-permute-start.3 = (f32[32,8,128]{2,1,0:T(8,128)S(1)}, f32[32,8,128]{2,1,0:T(8,128)S(1)}, u32[]{:S(2)}, u32[]{:S(2)}) collective-permute-start(f32[32,8,128]{2,1,0:T(8,128)S(1)} %get-tuple-element.19), channel_id=1, source_target_pairs={{1,0},{2,1},{3,2},{5,4},{6,5},{7,6},{9,8},{10,9},{11,10},{13,12},{... | collective-permute-start | bytes 393224 | tf_op jit(solution)/shard_map/ppermute | solution.py:293

commit v2 on v1

v2 whole, which is shorter than its diff:
```python
import jax
import jax.numpy as jnp
import numpy as np
from jax import lax
from jax.experimental import pallas as pl
from jax.experimental.pallas import tpu as pltpu
from jax.sharding import PartitionSpec as P

RADIUS = 8
TAPS = RADIUS + 1
UNIT = 1.0 / float(TAPS**2)
sharpness = 8.0
threshold = 0.5

GROUPS = 4
SLABS = 32
DEEP = 4


def call(kernel, out_shape, limit=48 * 1024 * 1024, **more):
    return pl.pallas_call(
        kernel,
        out_shape=out_shape,
        compiler_params=pltpu.CompilerParams(vmem_limit_bytes=limit),
        **more,
    )


def in_hbm(value):
    return pltpu.with_memory_space_constraint(value, pltpu.HBM)


def whole(count):
    return [pl.BlockSpec(memory_space=pltpu.VMEM)] * count


def hat(a, b):
    return jnp.maximum(TAPS - jnp.abs(a - b), 0)


def bf(value):
    return value.astype(jnp.bfloat16)


def f32(value):
    return value.astype(jnp.float32)


def parts_of(value, count):
    out = []
    for _ in range(count):
        part = bf(value)
        out.append(part)
        value = value - f32(part)
    return out


def dot(a, b, dims):
    return lax.dot_general(a, b, (dims, ((), ())), preferred_element_type=jnp.float32)


def iota(shape, dim):
    return lax.broadcasted_iota(jnp.int32, shape, dim)


def sensitivity_kernel(fwd_ref, adj_ref, weight_ref, terms_ref, fwd, adj, sems):
    copies = []
    for group in range(GROUPS):
        for which, (source, target) in enumerate(((fwd_ref, fwd), (adj_ref, adj))):
            piece = source.at[0, :, :, pl.ds(8 * group, 8)]
            copies.append(pltpu.make_async_copy(piece, target.at[group], sems.at[2 * group + which]))
            copies[-1].start()
    low = iota((8, 128), 0) < DEEP
    for pair in range(2):
        sides = []
        for group in (2 * pair, 2 * pair + 1):
            copies[2 * group].wait()
            copies[2 * group + 1].wait()
            total = None
            for component in range(3):
                real = f32(fwd[group, 0, component]) * f32(adj[group, 0, component])
                imag = f32(fwd[group, 1, component]) * f32(adj[group, 1, component])
                total = real - imag if total is None else total + (real - imag)
            sides.append((total * weight_ref[0]).reshape(128, 128))
        even, odd = (side.T.reshape(16, 8, 128) for side in sides)
        first = jnp.where(low, even, pltpu.roll(odd, DEEP, 1))
        second = jnp.where(low, pltpu.roll(even, DEEP, 1), odd)
        tiles = jnp.stack([first, second], axis=1).reshape(SLABS, 8, 128)
        terms_ref[:, 8 * pair : 8 * pair + 8, :] = tiles


def sensitivity(fwd, adj, weight):
    hbm = pl.BlockSpec(memory_space=pltpu.HBM)
    held = pltpu.VMEM((GROUPS, 2, 3, 8, 16, 128), jnp.bfloat16)
    return call(
        sensitivity_kernel,
        jax.ShapeDtypeStruct((SLABS, 16, 128), jnp.float32),
        in_specs=[hbm, hbm, pl.BlockSpec(memory_space=pltpu.SMEM)],
        out_specs=whole(1)[0],
        scratch_shapes=[held, held, pltpu.SemaphoreType.DMA((2 * GROUPS,))],
    )(in_hbm(fwd), in_hbm(adj), weight)


def middle_kernel(terms_ref, d_ref, m_ref, v_ref, out_ref, near_ref, far_ref):
    slab = lax.axis_index("illum")
    rows, cols = iota((8, 256), 0), iota((8, 256), 1)
    near = hat(slab * DEEP + (rows & 3), cols & 127)
    band = bf(jnp.where(((rows >> 2) & 1) == (cols >> 7), near, 0).astype(jnp.float32))
    own = []
    for pair in range(2):
        dens = d_ref[16 * pair : 16 * pair + 16].reshape(256, 128)
        dens = jnp.concatenate([dens[:128], dens[128:]], axis=1)
        own.append(sum(dot(band, part, ((1,), (1,))) for part in parts_of(dens, 2)))
    both = jnp.concatenate([jnp.sum(terms_ref[...], axis=0)] + own, axis=0)
    out_ref[...] = jnp.broadcast_to(both[None], out_ref.shape)
    near_at = pl.multiple_of(24 * (1 - (lax.axis_index("gx") & 1)), 8)
    for k, ref in enumerate((d_ref, m_ref, v_ref)):
        near_ref[k] = ref[pl.ds(near_at, 8)]
        far_ref[k] = ref[pl.ds(24 - near_at, 8)]


def middle(terms, density, moment_one, moment_two):
    edge = jax.ShapeDtypeStruct((3, 8, 16, 128), jnp.float32)
    return call(
        middle_kernel,
        (jax.ShapeDtypeStruct((16, 32, 128), jnp.float32), edge, edge),
        in_specs=whole(4),
        out_specs=tuple(whole(3)),
    )(terms, density, moment_one, moment_two)


def plane_taps():
    dx, dy, x, y = np.meshgrid(np.arange(-1, 2), np.arange(-1, 2), np.arange(8), np.arange(16), indexing="ij")
    far_x = (x + 8 * dx).reshape(-1, 1) - np.repeat(np.arange(8), 16)
    far_y = (y + 16 * dy).reshape(-1, 1) - np.tile(np.arange(16), 8)
    taps = np.maximum(TAPS - np.abs(far_x), 0) * np.maximum(TAPS - np.abs(far_y), 0)
    return jnp.asarray(taps.astype(np.float32)).astype(jnp.bfloat16)


PAD_X, PAD_Y = 3, 2


def slab_kernel(all_ref, taps_ref, out_ref, sens, dens):
    gx, gy = lax.axis_index("gx"), lax.axis_index("gy")
    low = iota((8, 128), 0) < DEEP
    zero = jnp.zeros((8, 128), jnp.float32)
    for ref in (sens, dens):
        for x in range(16 + 2 * PAD_X):
            for y in range(4 + 2 * PAD_Y):
                if not (PAD_X <= x < 16 + PAD_X and PAD_Y <= y < 4 + PAD_Y):
                    ref[x, y] = zero
    for x in range(4):
        for y in range(4):
            for pair in range(2):
                at = PAD_X + 4 * x + 2 * pair
                for ref, base in ((sens, 0), (dens, 16)):
                    tile = all_ref[4 * x + y, base + 8 * pair : base + 8 * pair + 8, :]
                    turned = pltpu.roll(tile, DEEP, 0)
                    twice = (jnp.where(low, tile, turned), jnp.where(low, turned, tile))
                    for odd in range(2):
                        value = twice[odd]
                        if base:
                            top = f32(bf(value))
                            value = jnp.where(low, top, value - top)
                        ref[at + odd, PAD_Y + y] = value
    taps = taps_ref[...]
    first = GROUPS * gx
    window = dens[pl.ds(first, 10), pl.ds(gy, 5)]
    side = jnp.concatenate(
        [bf(window[dx : dx + 8, dy : dy + 3].reshape(192, 128)) for dx in range(3) for dy in range(3)], axis=1
    )
    filtered = dot(side, taps, ((1,), (0,))).reshape(24, 8, 128)
    filtered = (filtered + pltpu.roll(filtered, DEEP, 1)) * (UNIT * UNIT * UNIT)
    inner = jnp.tanh(sharpness * (filtered - threshold))
    scale = jnp.tanh(jnp.full((8, 128), sharpness * threshold, jnp.float32)) * 2.0
    slope = sharpness * (1.0 - inner * inner) / scale
    chained = slope * sens[pl.ds(first + 1, 8), pl.ds(gy + 1, 3)].reshape(24, 8, 128)
    top = f32(bf(chained))
    chained = bf(jnp.where(low, top, chained - top)).reshape(8, 3, 8, 128)
    side = jnp.concatenate([chained[dx : dx + 6, dy].reshape(48, 128) for dx in range(3) for dy in range(3)], axis=1)
    result = dot(side, taps, ((1,), (0,))).reshape(6, 8, 128)
    result = result + pltpu.roll(result, DEEP, 1)
    for pair in range(3):
        tile = jnp.where(low, result[2 * pair], result[2 * pair + 1])
        out_ref[:, 8 * pair : 8 * pair + 8, :] = jnp.broadcast_to(tile[None], (SLABS, 8, 128))


def slab_step(everything):
    return call(
        slab_kernel,
        jax.ShapeDtypeStruct((SLABS, 24, 128), jnp.float32),
        in_specs=whole(2),
        out_specs=whole(1)[0],
        scratch_shapes=[pltpu.VMEM((16 + 2 * PAD_X, 4 + 2 * PAD_Y, 8, 128), jnp.float32)] * 2,
    )(everything, plane_taps())


def adam(density, moment_one, moment_two, gradient):
    new_one = 0.9 * moment_one + 0.1 * gradient
    new_two = 0.999 * moment_two + 0.001 * gradient * gradient
    first_fix = 1.0 - 0.9**5
    second_fix = 1.0 - 0.999**5
    step = new_one / first_fix / (jnp.sqrt(new_two / second_fix) + 1e-08)
    return jnp.clip(density - 0.05 * step, 0.0, 1.0), new_one, new_two


def box(value):
    n = value.shape[0]
    two = value[: n - 1] + value[1:]
    four = two[: n - 3] + two[2:]
    eight = four[: n - 7] + four[4:]
    return eight[: n - 8] + value[8:]


def adam_kernel(slabs_ref, d_ref, m_ref, v_ref, near_ref, far_ref, nd_ref, nm_ref, nv_ref, fx_ref, ynear_ref, yfar_ref, ext):
    gx, gy = lax.axis_index("gx"), lax.axis_index("gy")
    even_x, even_y = (gx & 1) == 0, (gy & 1) == 0
    rows, cols = iota((256, 256), 0), iota((256, 256), 1)
    depth = (rows >> 3) * DEEP + (rows & 3)
    near = jnp.where(((rows >> 2) & 1) == (cols >> 7), hat(depth, cols & 127), 0)
    band = bf(near.astype(jnp.float32))
    for pair in range(3):
        side = slabs_ref[:, 8 * pair : 8 * pair + 8, :].reshape(256, 128)
        both = sum(dot(part, band, ((0,), (0,))) for part in parts_of(side, 2)) * (UNIT * UNIT * UNIT)
        for odd in range(2):
            group = 2 * pair + odd - 1
            gradient = both[:, 128 * odd : 128 * odd + 128].reshape(8, 16, 128)
            if group == -1:
                left = [jnp.where(even_x, far_ref[k], near_ref[k]) for k in range(3)]
                new, _, _ = adam(*left, gradient)
                new = jnp.where(gx > 0, new, 0.0)
            elif group == GROUPS:
                right = [jnp.where(even_x, near_ref[k], far_ref[k]) for k in range(3)]
                new, _, _ = adam(*right, gradient)
                new = jnp.where(gx < lax.axis_size("gx") - 1, new, 0.0)
            else:
                at = slice(8 * group, 8 * group + 8)
                new, one, two = adam(d_ref[at], m_ref[at], v_ref[at], gradient)
                nd_ref[at] = new
                nm_ref[at] = one
                nv_ref[at] = two
            ext[8 * (group + 1) : 8 * (group + 1) + 8] = new
    along_x = box(box(ext[...])) * UNIT
    fx_ref[...] = along_x
    low, high = along_x[:, :8], along_x[:, 8:]
    ynear_ref[...] = jnp.where(even_y, high, low)
    yfar_ref[...] = jnp.where(even_y, low, high)


def adam_step(slabs, density, moment_one, moment_two, near, far):
    tile = jax.ShapeDtypeStruct((32, 16, 128), jnp.float32)
    half = jax.ShapeDtypeStruct((32, 8, 128), jnp.float32)
    return call(
        adam_kernel,
        (tile, tile, tile, tile, half, half),
        in_specs=whole(6),
        out_specs=tuple(whole(6)),
        scratch_shapes=[pltpu.VMEM((48, 16, 128), jnp.float32)],
    )(slabs, density, moment_one, moment_two, near, far)


def yz_filter(spread, sides):
    band = bf(hat(iota((128, 128), 0), iota((128, 128), 1)).astype(jnp.float32))
    side = jnp.concatenate(sides, axis=1)
    both = sum(dot(spread, part, ((1,), (0,))) for part in parts_of(side, 2))
    for odd in range(2):
        along_y = both[:, 128 * odd : 128 * odd + 128]
        yield sum(dot(part, band, ((1,), (0,))) for part in parts_of(along_y, 2)) * (UNIT * UNIT)


def own_kernel(fx_ref, nd_ref, nm_ref, nv_ref, own_ref, nd_out, nm_out, nv_out, sems):
    copies = [
        pltpu.make_async_copy(source, target, sems.at[k])
        for k, (source, target) in enumerate(((nd_ref, nd_out), (nm_ref, nm_out), (nv_ref, nv_out)))
    ]
    for copy in copies:
        copy.start()
    rows, cols = iota((128, 128), 0), iota((128, 128), 1)
    spread = bf(jnp.where((rows >> 4) == (cols >> 4), hat(rows & 15, cols & 15), 0).astype(jnp.float32))
    for pair in range(2):
        groups = [slice(8 * g, 8 * g + 8) for g in (2 * pair, 2 * pair + 1)]
        values = yz_filter(spread, [fx_ref[at].reshape(128, 128) for at in groups])
        for at, value in zip(groups, values):
            own_ref[at] = value.reshape(8, 16, 128)
    for copy in copies:
        copy.wait()


def own_step(along_x, *results):
    tile = jax.ShapeDtypeStruct((32, 16, 128), jnp.float32)
    return call(
        own_kernel,
        (tile, tile, tile, tile),
        in_specs=whole(4),
        out_specs=tuple(whole(1) + [pl.BlockSpec(memory_space=pltpu.HBM)] * 3),
        scratch_shapes=[pltpu.SemaphoreType.DMA((3,))],
    )(along_x, *results)


def physical_kernel(own_ref, near_ref, far_ref, out_ref, held, sems):
    even = (lax.axis_index("gy") & 1) == 0
    rows, cols = iota((128, 128), 0), iota((128, 128), 1)
    later = (cols < 64) == even
    y = (cols & 7) + jnp.where(later, 16, -8)
    spread = bf(jnp.where(((cols & 63) >> 3) == (rows >> 4), hat(y, rows & 15), 0).astype(jnp.float32))
    scale = jnp.tanh(jnp.full((128, 128), sharpness * threshold, jnp.float32))
    copies = []
    for pair in range(2):
        groups = [slice(8 * g, 8 * g + 8) for g in (2 * pair, 2 * pair + 1)]
        sides = [jnp.concatenate([near_ref[at].reshape(64, 128), far_ref[at].reshape(64, 128)], axis=0) for at in groups]
        for at, value in zip(groups, yz_filter(spread, sides)):
            value = value + own_ref[at].reshape(128, 128)
            value = (scale + jnp.tanh(sharpness * (value - threshold))) / (scale + scale)
            held[at] = value.reshape(8, 16, 128)
            copies.append(pltpu.make_async_copy(held.at[at], out_ref.at[at], sems.at[len(copies)]))
            copies[-1].start()
    for copy in copies:
        copy.wait()


def physical_step(own, near, far):
    return call(
        physical_kernel,
        jax.ShapeDtypeStruct((32, 16, 128), jnp.float32),
        in_specs=whole(3),
        out_specs=pl.BlockSpec(memory_space=pltpu.HBM),
        scratch_shapes=[pltpu.VMEM((32, 16, 128), jnp.float32), pltpu.SemaphoreType.DMA((GROUPS,))],
    )(own, near, far)


def swap(near, far, axis):
    size = lax.axis_size(axis)
    pairs = [(i, i ^ 1) for i in range(size)]
    others = [(i, j) for k in range(1, size - 1, 2) for i, j in ((k, k + 1), (k + 1, k))]
    return lax.ppermute(near, axis, pairs), lax.ppermute(far, axis, others)


def exchange(value, axes):
    return lax.all_to_all(value, axes, 0, 0, tiled=True)


def shards(density, moment_one, moment_two, forward_field, adjoint_field, objective_weight):
    state = (density, moment_one, moment_two)
    terms = exchange(sensitivity(forward_field, adjoint_field, objective_weight), "illum")
    both, near, far = middle(terms, *state)
    slab = slab_step(exchange(both, ("gx", "gy")))
    slab, near, far = lax.optimization_barrier((slab, near, far))
    slabs = exchange(slab, "illum")
    near, far = swap(near, far, "gx")
    *results, along_x, near, far = adam_step(slabs, *state, near, far)
    near, far = swap(near, far, "gy")
    own, *results = own_step(along_x, *results)
    return (*results, physical_step(own, near, far))


def solution(mesh):
    tile = P("gx", "gy", None)
    field = P("illum", None, None, "gx", "gy", None)
    return jax.shard_map(
        shards,
        mesh=mesh,
        in_specs=(tile, tile, tile, field, field, P("illum")),
        out_specs=(tile, tile, tile, tile),
        check_vma=False,
    )
```

time: 85.4 us -> 81.4 us (0.953)
  local copies, waits for them, and re-layouts: 3.23 us -> 0.03 us
  starting transfers between devices: 16.8 us -> 14.3 us
  waiting for transfers between devices: 13.6 us -> 14.8 us
    unnamed x14 -> x8, local copies, waits for them, and re-layouts: 3.23 us -> 0.03 us
    ppermute x4, starting transfers between devices: 12.8 us -> 10.4 us  [swap(): return (lax.ppermute(near, axis, pairs), lax.ppermute(far, axis, others))]
    pallas_call x2 -> x3, Pallas kernels: 1.05 us -> 2.78 us  [the longest x1 1.69 us: sensitivity(): call(sensitivity_kernel, jax.ShapeDtypeStruct((SLABS, 16, 128), jnp.float...]
    all_to_all x1, waiting for transfers between devices: 6.36 us -> 7.32 us  [exchange(): return lax.all_to_all(value, axes, 0, 0, tiled=True)]
  transfers between devices with their start and end apart: 5 -> 5, of which waited for: 4 -> 3; matrix products, arithmetic and copies ran while one was open for 0% -> 0% of each run, Pallas kernels for 0% -> 1%
where the time goes in v2:
time: 81.4 us; the launch traced here: 81 us
  blocking collectives  44.6 us (55%)
  waiting for transfers between devices  14.8 us (18%)
  starting transfers between devices  14.3 us (18%)
  Pallas kernels  5.98 us (7%)
  between operations  1.39 us (2%)
    all_to_all x2, blocking collectives, exchange(): return lax.all_to_all(value, axes, 0, 0, tiled=True)  44.6 us
    ppermute x4, starting transfers between devices, swap(): return (lax.ppermute(near, axis, pairs), lax.ppermute(far, axis, others))  10.4 us
    ppermute x4, waiting for transfers between devices, swap(): return (lax.ppermute(near, axis, pairs), lax.ppermute(far, axis, others))  7.43 us
    all_to_all x1, waiting for transfers between devices, exchange(): return lax.all_to_all(value, axes, 0, 0, tiled=True)  7.32 us
    all_to_all x1, starting transfers between devices, exchange(): return lax.all_to_all(value, axes, 0, 0, tiled=True)  3.88 us
    pallas_call x1, Pallas kernels, sensitivity(): call(sensitivity_kernel, jax.ShapeDtypeStruct((SLABS, 16, 128), jnp.float...  1.69 us
  transfers between devices with their start and end apart: 5, of which 3 were waited for; matrix products, arithmetic and copies ran while one was open for 0% of the time, Pallas kernels for 1%

profile of v2, /device:TPU:1, one launch (start us, length us, event | category | flops | bytes accessed | tf_op | source)
XLA Modules:
  0.0 81.0 jit_solution(13110402984182931433)
XLA Ops:
  1.3 0.0 copy-start.2
  1.3 1.7 %shard_map.102 = f32[32,16,128]{2,1,0:T(8,128)S(1)} custom-call(bf16[1,2,3,32,16,128]{5,4,3,2,1,0:T(8,128)(2,1)} %fwd_ref.1, bf16[1,2,3,32,16,128]{5,4,3,2,1,0:T(8,128)(2,1)} %adj_ref.1, f32[1]{0:T(128)S(6)} %copy.11.weight_ref), custom_call_target="tpu_custom_call" | custom-call | tf_op jit(solution)/shard_map/pallas_call | solution.py:95
  3.0 0.0 copy-start
  3.0 0.0 copy-start.1
  3.0 29.1 %all_to_all.15.terms_ref = f32[32,16,128]{2,1,0:T(8,128)S(1)} all-to-all(f32[32,16,128]{2,1,0:T(8,128)S(1)} %shard_map.102), channel_id=1, replica_groups=mesh['illum'=32,'gx'=4,'gy'=4] {'illum'}, dimensions={0} | all-to-all | bytes 524288 | tf_op jit(solution)/shard_map/all_to_all | solution.py:339
  32.1 0.0 copy-done.2
  32.1 0.0 copy-done
  32.1 0.0 copy-done.1
  32.1 0.2 shard_map.103
  32.3 0.0 copy-start.3
  32.3 15.5 %all_to_all.16.all_ref = f32[16,32,128]{2,1,0:T(8,128)S(1)} all-to-all(f32[16,32,128]{2,1,0:T(8,128)S(1)} %get-tuple-element.20), channel_id=1, replica_groups=mesh['illum'=32,'gx'=4,'gy'=4] {'gx','gy'}, dimensions={0} | all-to-all | bytes 524288 | tf_op jit(solution)/shard_map/all_to_all | solution.py:339
  47.8 0.0 copy-done.3
  47.8 1.3 %shard_map.104 = f32[32,24,128]{2,1,0:T(8,128)} custom-call(f32[16,32,128]{2,1,0:T(8,128)S(1)} %all_to_all.16.all_ref, bf16[1152,128]{1,0:T(8,128)(2,1)S(1)} %copy-done.3), custom_call_target="tpu_custom_call" | custom-call | tf_op jit(solution)/shard_map/pallas_call | solution.py:189
  49.1 3.9 %all-to-all-start.2 = ((f32[32,24,128]{2,1,0:T(8,128)}), f32[32,24,128]{2,1,0:T(8,128)S(1)}, u32[]{:S(2)}, u32[]{:S(2)}) async-start(f32[32,24,128]{2,1,0:T(8,128)} %shard_map.104), calls=%async_computation.2 | async-start | bytes 786432 | tf_op jit(solution)/shard_map/all_to_all | solution.py:339
  53.0 2.2 %collective-permute-start = (f32[3,8,16,128]{3,2,1,0:T(8,128)S(1)}, f32[3,8,16,128]{3,2,1,0:T(8,128)S(1)}, u32[]{:S(2)}, u32[]{:S(2)}) collective-permute-start(f32[3,8,16,128]{3,2,1,0:T(8,128)S(1)} %get-tuple-element.24), channel_id=1, source_target_pairs={{0,4},{4,0},{8,12},{12,8},{1,5},{5,1},{9,13},{13,9},{2,6},{6,2},{1... | collective-permute-start | bytes 589832 | tf_op jit(solution)/shard_map/ppermute | solution.py:335
  55.2 0.7 collective-permute-start.1
  55.9 4.4 %collective-permute-done.near_ref = f32[3,8,16,128]{3,2,1,0:T(8,128)S(1)} collective-permute-done((f32[3,8,16,128]{3,2,1,0:T(8,128)S(1)}, f32[3,8,16,128]{3,2,1,0:T(8,128)S(1)}, u32[]{:S(2)}, u32[]{:S(2)}) %collective-permute-start) | collective-permute-done | bytes 196640 | tf_op jit(solution)/shard_map/ppermute | solution.py:335
  60.4 0.0 collective-permute-done.1.far_ref
  60.4 7.3 %all-to-all-done.2.slabs_ref = f32[32,24,128]{2,1,0:T(8,128)S(1)} async-done(((f32[32,24,128]{2,1,0:T(8,128)}), f32[32,24,128]{2,1,0:T(8,128)S(1)}, u32[]{:S(2)}, u32[]{:S(2)}) %all-to-all-start.2) | async-done | bytes 393248 | tf_op jit(solution)/shard_map/all_to_all | solution.py:339
  67.7 0.8 shard_map.105
  68.4 5.1 %collective-permute-start.2 = (f32[32,8,128]{2,1,0:T(8,128)S(1)}, f32[32,8,128]{2,1,0:T(8,128)S(1)}, u32[]{:S(2)}, u32[]{:S(2)}) collective-permute-start(f32[32,8,128]{2,1,0:T(8,128)S(1)} %get-tuple-element.34), channel_id=1, source_target_pairs={{0,1},{1,0},{2,3},{3,2},{4,5},{5,4},{6,7},{7,6},{8,9},{9,8},{10,11... | collective-permute-start | bytes 393224 | tf_op jit(solution)/shard_map/ppermute | solution.py:335
  73.6 2.4 %collective-permute-start.3 = (f32[32,8,128]{2,1,0:T(8,128)S(1)}, f32[32,8,128]{2,1,0:T(8,128)S(1)}, u32[]{:S(2)}, u32[]{:S(2)}) collective-permute-start(f32[32,8,128]{2,1,0:T(8,128)S(1)} %get-tuple-element.35), channel_id=1, source_target_pairs={{1,2},{2,1},{5,6},{6,5},{9,10},{10,9},{13,14},{14,13},{17,18},{18,... | collective-permute-start | bytes 393224 | tf_op jit(solution)/shard_map/ppermute | solution.py:335
  76.0 0.9 %shard_map.106 = (f32[32,16,128]{2,1,0:T(8,128)S(1)}, f32[32,16,128]{2,1,0:T(8,128)}, f32[32,16,128]{2,1,0:T(8,128)}, f32[32,16,128]{2,1,0:T(8,128)}) custom-call(f32[32,16,128]{2,1,0:T(8,128)S(1)} %get-tuple-element.26.fx_ref, f32[32,16,128]{2,1,0:T(8,128)S(1)} %get-tuple-element.27.nd_ref, f32[32,16,128]{2,1,0:T(8,128)S(1)} %get-tuple-element.28.nm_ref, ...), custom_call_target="tpu_custom_call" | custom-call | tf_op jit(solution)/shard_map/pallas_call | solution.py:291
  76.9 0.0 collective-permute-done.2.near_ref
  76.9 3.0 %collective-permute-done.3.far_ref = f32[32,8,128]{2,1,0:T(8,128)S(1)} collective-permute-done((f32[32,8,128]{2,1,0:T(8,128)S(1)}, f32[32,8,128]{2,1,0:T(8,128)S(1)}, u32[]{:S(2)}, u32[]{:S(2)}) %collective-permute-start.3) | collective-permute-done | bytes 131104 | tf_op jit(solution)/shard_map/ppermute | solution.py:335
  79.9 1.1 %shard_map.107 = f32[32,16,128]{2,1,0:T(8,128)} custom-call(f32[32,16,128]{2,1,0:T(8,128)S(1)} %get-tuple-element.33.own_ref, f32[32,8,128]{2,1,0:T(8,128)S(1)} %collective-permute-done.2.near_ref, f32[32,8,128]{2,1,0:T(8,128)S(1)} %collective-permute-done.3.far_ref), custom_call_target="tpu_custom_call" | custom-call | tf_op jit(solution)/shard_map/pallas_call | solution.py:322
Async XLA Ops:
  1.3 30.8 %copy-start.2 = (f32[32,16,128]{2,1,0:T(8,128)S(1)}, f32[32,16,128]{2,1,0:T(8,128)}, u32[]{:S(2)}) copy-start(f32[32,16,128]{2,1,0:T(8,128)} %v_ref.3) | copy-start | bytes 786436
  3.0 29.1 %copy-start = (f32[32,16,128]{2,1,0:T(8,128)S(1)}, f32[32,16,128]{2,1,0:T(8,128)}, u32[]{:S(2)}) copy-start(f32[32,16,128]{2,1,0:T(8,128)} %d_ref.3) | copy-start | bytes 786436
  3.0 29.1 %copy-start.1 = (f32[32,16,128]{2,1,0:T(8,128)S(1)}, f32[32,16,128]{2,1,0:T(8,128)}, u32[]{:S(2)}) copy-start(f32[32,16,128]{2,1,0:T(8,128)} %m_ref.3) | copy-start | bytes 786436
  32.3 15.5 %copy-start.3 = (bf16[1152,128]{1,0:T(8,128)(2,1)S(1)}, bf16[1152,128]{1,0:T(8,128)(2,1)}, u32[]{:S(2)}) copy-start(bf16[1152,128]{1,0:T(8,128)(2,1)} %constant.6.taps_ref) | copy-start | bytes 884740
  49.1 18.5 %all-to-all-start.2 = ((f32[32,24,128]{2,1,0:T(8,128)}), f32[32,24,128]{2,1,0:T(8,128)S(1)}, u32[]{:S(2)}, u32[]{:S(2)}) async-start(f32[32,24,128]{2,1,0:T(8,128)} %shard_map.104), calls=%async_computation.2 | async-start | bytes 786432 | tf_op jit(solution)/shard_map/all_to_all | solution.py:339
  53.0 7.3 %collective-permute-start = (f32[3,8,16,128]{3,2,1,0:T(8,128)S(1)}, f32[3,8,16,128]{3,2,1,0:T(8,128)S(1)}, u32[]{:S(2)}, u32[]{:S(2)}) collective-permute-start(f32[3,8,16,128]{3,2,1,0:T(8,128)S(1)} %get-tuple-element.24), channel_id=1, source_target_pairs={{0,4},{4,0},{8,12},{12,8},{1,5},{5,1},{9,13},{13,9},{2,6},{6,2},{1... | collective-permute-start | bytes 589832 | tf_op jit(solution)/shard_map/ppermute | solution.py:335
  55.2 5.1 %collective-permute-start.1 = (f32[3,8,16,128]{3,2,1,0:T(8,128)S(1)}, f32[3,8,16,128]{3,2,1,0:T(8,128)S(1)}, u32[]{:S(2)}, u32[]{:S(2)}) collective-permute-start(f32[3,8,16,128]{3,2,1,0:T(8,128)S(1)} %get-tuple-element.25), channel_id=1, source_target_pairs={{4,8},{8,4},{5,9},{9,5},{6,10},{10,6},{7,11},{11,7},{20,24},{24,20... | collective-permute-start | bytes 589832 | tf_op jit(solution)/shard_map/ppermute | solution.py:335
  68.4 8.4 %collective-permute-start.2 = (f32[32,8,128]{2,1,0:T(8,128)S(1)}, f32[32,8,128]{2,1,0:T(8,128)S(1)}, u32[]{:S(2)}, u32[]{:S(2)}) collective-permute-start(f32[32,8,128]{2,1,0:T(8,128)S(1)} %get-tuple-element.34), channel_id=1, source_target_pairs={{0,1},{1,0},{2,3},{3,2},{4,5},{5,4},{6,7},{7,6},{8,9},{9,8},{10,11... | collective-permute-start | bytes 393224 | tf_op jit(solution)/shard_map/ppermute | solution.py:335
  73.6 6.3 %collective-permute-start.3 = (f32[32,8,128]{2,1,0:T(8,128)S(1)}, f32[32,8,128]{2,1,0:T(8,128)S(1)}, u32[]{:S(2)}, u32[]{:S(2)}) collective-permute-start(f32[32,8,128]{2,1,0:T(8,128)S(1)} %get-tuple-element.35), channel_id=1, source_target_pairs={{1,2},{2,1},{5,6},{6,5},{9,10},{10,9},{13,14},{14,13},{17,18},{18,... | collective-permute-start | bytes 393224 | tf_op jit(solution)/shard_map/ppermute | solution.py:335

commit v3 on v2

--- a/solution.py
+++ b/solution.py
@@ -297,7 +297,7 @@
     )(along_x, *results)
 
 
-def physical_kernel(own_ref, near_ref, far_ref, out_ref, held, sems):
+def physical_kernel(far_ref, own_ref, near_ref, out_ref, held, sems):
     even = (lax.axis_index("gy") & 1) == 0
     rows, cols = iota((128, 128), 0), iota((128, 128), 1)
     later = (cols < 64) == even
@@ -325,14 +325,15 @@
         in_specs=whole(3),
         out_specs=pl.BlockSpec(memory_space=pltpu.HBM),
         scratch_shapes=[pltpu.VMEM((32, 16, 128), jnp.float32), pltpu.SemaphoreType.DMA((GROUPS,))],
-    )(own, near, far)
+    )(far, own, near)
 
 
 def swap(near, far, axis):
     size = lax.axis_size(axis)
     pairs = [(i, i ^ 1) for i in range(size)]
     others = [(i, j) for k in range(1, size - 1, 2) for i, j in ((k, k + 1), (k + 1, k))]
-    return lax.ppermute(near, axis, pairs), lax.ppermute(far, axis, others)
+    far = lax.ppermute(far, axis, others)
+    return lax.ppermute(near, axis, pairs), far
 
 
 def exchange(value, axes):

time: 81.4 us -> 79 us (0.971)
  waiting for transfers between devices: 14.8 us -> 12.2 us
    ppermute x4, waiting for transfers between devices: 7.43 us -> 4.84 us  [the longest x2 4.83 us: swap(): return (lax.ppermute(near, axis, pairs), far)]
where the time goes in v3:
time: 79 us; the launch traced here: 78.4 us
  blocking collectives  44.6 us (56%)
  starting transfers between devices  14.3 us (18%)
  waiting for transfers between devices  12.2 us (15%)
  Pallas kernels  5.98 us (8%)
  between operations  1.39 us (2%)
    all_to_all x2, blocking collectives, exchange(): return lax.all_to_all(value, axes, 0, 0, tiled=True)  44.6 us
    all_to_all x1, waiting for transfers between devices, exchange(): return lax.all_to_all(value, axes, 0, 0, tiled=True)  7.32 us
    ppermute x2, starting transfers between devices, swap(): far = lax.ppermute(far, axis, others)  6.27 us
    ppermute x2, waiting for transfers between devices, swap(): return (lax.ppermute(near, axis, pairs), far)  4.83 us
    ppermute x2, starting transfers between devices, swap(): return (lax.ppermute(near, axis, pairs), far)  4.11 us
    all_to_all x1, starting transfers between devices, exchange(): return lax.all_to_all(value, axes, 0, 0, tiled=True)  3.88 us
    pallas_call x1, Pallas kernels, sensitivity(): call(sensitivity_kernel, jax.ShapeDtypeStruct((SLABS, 16, 128), jnp.float...  1.69 us
  transfers between devices with their start and end apart: 5, of which 3 were waited for; matrix products, arithmetic and copies ran while one was open for 0% of the time, Pallas kernels for 1%

profile of v3, /device:TPU:1, one launch (start us, length us, event | category | flops | bytes accessed | tf_op | source)
XLA Modules:
  0.0 78.4 jit_solution(13016870350702422178)
XLA Ops:
  1.3 0.0 copy-start.2
  1.3 1.7 %shard_map.102 = f32[32,16,128]{2,1,0:T(8,128)S(1)} custom-call(bf16[1,2,3,32,16,128]{5,4,3,2,1,0:T(8,128)(2,1)} %fwd_ref.1, bf16[1,2,3,32,16,128]{5,4,3,2,1,0:T(8,128)(2,1)} %adj_ref.1, f32[1]{0:T(128)S(6)} %copy.11.weight_ref), custom_call_target="tpu_custom_call" | custom-call | tf_op jit(solution)/shard_map/pallas_call | solution.py:95
  3.0 0.0 copy-start
  3.0 0.0 copy-start.1
  3.0 29.1 %all_to_all.15.terms_ref = f32[32,16,128]{2,1,0:T(8,128)S(1)} all-to-all(f32[32,16,128]{2,1,0:T(8,128)S(1)} %shard_map.102), channel_id=1, replica_groups=mesh['illum'=32,'gx'=4,'gy'=4] {'illum'}, dimensions={0} | all-to-all | bytes 524288 | tf_op jit(solution)/shard_map/all_to_all | solution.py:340
  32.1 0.0 copy-done.2
  32.1 0.0 copy-done
  32.1 0.0 copy-done.1
  32.1 0.2 shard_map.103
  32.3 0.0 copy-start.3
  32.3 15.5 %all_to_all.16.all_ref = f32[16,32,128]{2,1,0:T(8,128)S(1)} all-to-all(f32[16,32,128]{2,1,0:T(8,128)S(1)} %get-tuple-element.20), channel_id=1, replica_groups=mesh['illum'=32,'gx'=4,'gy'=4] {'gx','gy'}, dimensions={0} | all-to-all | bytes 524288 | tf_op jit(solution)/shard_map/all_to_all | solution.py:340
  47.8 0.0 copy-done.3
  47.8 1.3 %shard_map.104 = f32[32,24,128]{2,1,0:T(8,128)} custom-call(f32[16,32,128]{2,1,0:T(8,128)S(1)} %all_to_all.16.all_ref, bf16[1152,128]{1,0:T(8,128)(2,1)S(1)} %copy-done.3), custom_call_target="tpu_custom_call" | custom-call | tf_op jit(solution)/shard_map/pallas_call | solution.py:189
  49.1 3.9 %all-to-all-start.2 = ((f32[32,24,128]{2,1,0:T(8,128)}), f32[32,24,128]{2,1,0:T(8,128)S(1)}, u32[]{:S(2)}, u32[]{:S(2)}) async-start(f32[32,24,128]{2,1,0:T(8,128)} %shard_map.104), calls=%async_computation.2 | async-start | bytes 786432 | tf_op jit(solution)/shard_map/all_to_all | solution.py:340
  53.0 2.2 %collective-permute-start = (f32[3,8,16,128]{3,2,1,0:T(8,128)S(1)}, f32[3,8,16,128]{3,2,1,0:T(8,128)S(1)}, u32[]{:S(2)}, u32[]{:S(2)}) collective-permute-start(f32[3,8,16,128]{3,2,1,0:T(8,128)S(1)} %get-tuple-element.24), channel_id=1, source_target_pairs={{0,4},{4,0},{8,12},{12,8},{1,5},{5,1},{9,13},{13,9},{2,6},{6,2},{1... | collective-permute-start | bytes 589832 | tf_op jit(solution)/shard_map/ppermute | solution.py:336
  55.2 0.7 collective-permute-start.1
  55.9 4.4 %collective-permute-done.near_ref = f32[3,8,16,128]{3,2,1,0:T(8,128)S(1)} collective-permute-done((f32[3,8,16,128]{3,2,1,0:T(8,128)S(1)}, f32[3,8,16,128]{3,2,1,0:T(8,128)S(1)}, u32[]{:S(2)}, u32[]{:S(2)}) %collective-permute-start) | collective-permute-done | bytes 196640 | tf_op jit(solution)/shard_map/ppermute | solution.py:336
  60.4 0.0 collective-permute-done.1.far_ref
  60.4 7.3 %all-to-all-done.2.slabs_ref = f32[32,24,128]{2,1,0:T(8,128)S(1)} async-done(((f32[32,24,128]{2,1,0:T(8,128)}), f32[32,24,128]{2,1,0:T(8,128)S(1)}, u32[]{:S(2)}, u32[]{:S(2)}) %all-to-all-start.2) | async-done | bytes 393248 | tf_op jit(solution)/shard_map/all_to_all | solution.py:340
  67.7 0.8 shard_map.105
  68.4 5.6 %collective-permute-start.2 = (f32[32,8,128]{2,1,0:T(8,128)S(1)}, f32[32,8,128]{2,1,0:T(8,128)S(1)}, u32[]{:S(2)}, u32[]{:S(2)}) collective-permute-start(f32[32,8,128]{2,1,0:T(8,128)S(1)} %get-tuple-element.33), channel_id=1, source_target_pairs={{1,2},{2,1},{5,6},{6,5},{9,10},{10,9},{13,14},{14,13},{17,18},{18,... | collective-permute-start | bytes 393224 | tf_op jit(solution)/shard_map/ppermute | solution.py:335
  74.0 1.9 %collective-permute-start.3 = (f32[32,8,128]{2,1,0:T(8,128)S(1)}, f32[32,8,128]{2,1,0:T(8,128)S(1)}, u32[]{:S(2)}, u32[]{:S(2)}) collective-permute-start(f32[32,8,128]{2,1,0:T(8,128)S(1)} %get-tuple-element.35), channel_id=1, source_target_pairs={{0,1},{1,0},{2,3},{3,2},{4,5},{5,4},{6,7},{7,6},{8,9},{9,8},{10,11... | collective-permute-start | bytes 393224 | tf_op jit(solution)/shard_map/ppermute | solution.py:336
  76.0 0.9 %shard_map.106 = (f32[32,16,128]{2,1,0:T(8,128)S(1)}, f32[32,16,128]{2,1,0:T(8,128)}, f32[32,16,128]{2,1,0:T(8,128)}, f32[32,16,128]{2,1,0:T(8,128)}) custom-call(f32[32,16,128]{2,1,0:T(8,128)S(1)} %get-tuple-element.26.fx_ref, f32[32,16,128]{2,1,0:T(8,128)S(1)} %get-tuple-element.27.nd_ref, f32[32,16,128]{2,1,0:T(8,128)S(1)} %get-tuple-element.28.nm_ref, ...), custom_call_target="tpu_custom_call" | custom-call | tf_op jit(solution)/shard_map/pallas_call | solution.py:291
  76.9 0.0 collective-permute-done.2.far_ref
  76.9 0.4 collective-permute-done.3.near_ref
  77.3 1.1 %shard_map.107 = f32[32,16,128]{2,1,0:T(8,128)} custom-call(f32[32,8,128]{2,1,0:T(8,128)S(1)} %collective-permute-done.2.far_ref, f32[32,16,128]{2,1,0:T(8,128)S(1)} %get-tuple-element.34.own_ref, f32[32,8,128]{2,1,0:T(8,128)S(1)} %collective-permute-done.3.near_ref), custom_call_target="tpu_custom_call" | custom-call | tf_op jit(solution)/shard_map/pallas_call | solution.py:322
Async XLA Ops:
  1.3 30.8 %copy-start.2 = (f32[32,16,128]{2,1,0:T(8,128)S(1)}, f32[32,16,128]{2,1,0:T(8,128)}, u32[]{:S(2)}) copy-start(f32[32,16,128]{2,1,0:T(8,128)} %v_ref.3) | copy-start | bytes 786436
  3.0 29.1 %copy-start = (f32[32,16,128]{2,1,0:T(8,128)S(1)}, f32[32,16,128]{2,1,0:T(8,128)}, u32[]{:S(2)}) copy-start(f32[32,16,128]{2,1,0:T(8,128)} %d_ref.3) | copy-start | bytes 786436
  3.0 29.1 %copy-start.1 = (f32[32,16,128]{2,1,0:T(8,128)S(1)}, f32[32,16,128]{2,1,0:T(8,128)}, u32[]{:S(2)}) copy-start(f32[32,16,128]{2,1,0:T(8,128)} %m_ref.3) | copy-start | bytes 786436
  32.3 15.5 %copy-start.3 = (bf16[1152,128]{1,0:T(8,128)(2,1)S(1)}, bf16[1152,128]{1,0:T(8,128)(2,1)}, u32[]{:S(2)}) copy-start(bf16[1152,128]{1,0:T(8,128)(2,1)} %constant.6.taps_ref) | copy-start | bytes 884740
  49.1 18.5 %all-to-all-start.2 = ((f32[32,24,128]{2,1,0:T(8,128)}), f32[32,24,128]{2,1,0:T(8,128)S(1)}, u32[]{:S(2)}, u32[]{:S(2)}) async-start(f32[32,24,128]{2,1,0:T(8,128)} %shard_map.104), calls=%async_computation.2 | async-start | bytes 786432 | tf_op jit(solution)/shard_map/all_to_all | solution.py:340
  53.0 7.3 %collective-permute-start = (f32[3,8,16,128]{3,2,1,0:T(8,128)S(1)}, f32[3,8,16,128]{3,2,1,0:T(8,128)S(1)}, u32[]{:S(2)}, u32[]{:S(2)}) collective-permute-start(f32[3,8,16,128]{3,2,1,0:T(8,128)S(1)} %get-tuple-element.24), channel_id=1, source_target_pairs={{0,4},{4,0},{8,12},{12,8},{1,5},{5,1},{9,13},{13,9},{2,6},{6,2},{1... | collective-permute-start | bytes 589832 | tf_op jit(solution)/shard_map/ppermute | solution.py:336
  55.2 5.1 %collective-permute-start.1 = (f32[3,8,16,128]{3,2,1,0:T(8,128)S(1)}, f32[3,8,16,128]{3,2,1,0:T(8,128)S(1)}, u32[]{:S(2)}, u32[]{:S(2)}) collective-permute-start(f32[3,8,16,128]{3,2,1,0:T(8,128)S(1)} %get-tuple-element.25), channel_id=1, source_target_pairs={{4,8},{8,4},{5,9},{9,5},{6,10},{10,6},{7,11},{11,7},{20,24},{24,20... | collective-permute-start | bytes 589832 | tf_op jit(solution)/shard_map/ppermute | solution.py:335
  68.4 8.4 %collective-permute-start.2 = (f32[32,8,128]{2,1,0:T(8,128)S(1)}, f32[32,8,128]{2,1,0:T(8,128)S(1)}, u32[]{:S(2)}, u32[]{:S(2)}) collective-permute-start(f32[32,8,128]{2,1,0:T(8,128)S(1)} %get-tuple-element.33), channel_id=1, source_target_pairs={{1,2},{2,1},{5,6},{6,5},{9,10},{10,9},{13,14},{14,13},{17,18},{18,... | collective-permute-start | bytes 393224 | tf_op jit(solution)/shard_map/ppermute | solution.py:335
  74.0 3.2 %collective-permute-start.3 = (f32[32,8,128]{2,1,0:T(8,128)S(1)}, f32[32,8,128]{2,1,0:T(8,128)S(1)}, u32[]{:S(2)}, u32[]{:S(2)}) collective-permute-start(f32[32,8,128]{2,1,0:T(8,128)S(1)} %get-tuple-element.35), channel_id=1, source_target_pairs={{0,1},{1,0},{2,3},{3,2},{4,5},{5,4},{6,7},{7,6},{8,9},{9,8},{10,11... | collective-permute-start | bytes 393224 | tf_op jit(solution)/shard_map/ppermute | solution.py:336

commit v4 on v3

--- a/solution.py
+++ b/solution.py
@@ -102,7 +102,7 @@
 
 
 def middle_kernel(terms_ref, d_ref, m_ref, v_ref, out_ref, near_ref, far_ref):
-    slab = lax.axis_index("illum")
+    slab = SLABS - 1 - lax.axis_index("illum")
     rows, cols = iota((8, 256), 0), iota((8, 256), 1)
     near = hat(slab * DEEP + (rows & 3), cols & 127)
     band = bf(jnp.where(((rows >> 2) & 1) == (cols >> 7), near, 0).astype(jnp.float32))
@@ -336,17 +336,21 @@
     return lax.ppermute(near, axis, pairs), far
 
 
-def exchange(value, axes):
-    return lax.all_to_all(value, axes, 0, 0, tiled=True)
+def exchange(value, axes, groups=None):
+    return lax.all_to_all(value, axes, 0, 0, tiled=True, axis_index_groups=groups)
+
+
+def countdown(axis):
+    return [list(reversed(range(lax.axis_size(axis))))]
 
 
 def shards(density, moment_one, moment_two, forward_field, adjoint_field, objective_weight):
     state = (density, moment_one, moment_two)
-    terms = exchange(sensitivity(forward_field, adjoint_field, objective_weight), "illum")
+    terms = exchange(sensitivity(forward_field, adjoint_field, objective_weight), "illum", countdown("illum"))
     both, near, far = middle(terms, *state)
     slab = slab_step(exchange(both, ("gx", "gy")))
     slab, near, far = lax.optimization_barrier((slab, near, far))
-    slabs = exchange(slab, "illum")
+    slabs = exchange(slab, "illum", countdown("illum"))
     near, far = swap(near, far, "gx")
     *results, along_x, near, far = adam_step(slabs, *state, near, far)
     near, far = swap(near, far, "gy")

time: 79 us -> 74.4 us (0.942)
  blocking collectives: 44.6 us -> 39.1 us
  starting transfers between devices: 14.3 us -> 19.4 us
  waiting for transfers between devices: 12.2 us -> 8.14 us
    all_to_all x1, starting transfers between devices: 3.88 us -> 9.56 us  [exchange(): lax.all_to_all(value, axes, 0, 0, tiled=True, axis_index_groups=groups)]
    all_to_all x2, blocking collectives: 44.6 us -> 39.1 us  [exchange(): lax.all_to_all(value, axes, 0, 0, tiled=True, axis_index_groups=groups)]
    all_to_all x1, waiting for transfers between devices: 7.32 us -> 3.6 us  [exchange(): lax.all_to_all(value, axes, 0, 0, tiled=True, axis_index_groups=groups)]
where the time goes in v4:
time: 74.4 us; the launch traced here: 74 us
  blocking collectives  39.1 us (53%)
  starting transfers between devices  19.4 us (26%)
  waiting for transfers between devices  8.14 us (11%)
  Pallas kernels  5.98 us (8%)
  between operations  1.39 us (2%)
    all_to_all x2, blocking collectives, exchange(): lax.all_to_all(value, axes, 0, 0, tiled=True, axis_index_groups=groups)  39.1 us
    all_to_all x1, starting transfers between devices, exchange(): lax.all_to_all(value, axes, 0, 0, tiled=True, axis_index_groups=groups)  9.56 us
    ppermute x2, starting transfers between devices, swap(): far = lax.ppermute(far, axis, others)  5.72 us
    ppermute x2, waiting for transfers between devices, swap(): return (lax.ppermute(near, axis, pairs), far)  4.54 us
    ppermute x2, starting transfers between devices, swap(): return (lax.ppermute(near, axis, pairs), far)  4.11 us
    all_to_all x1, waiting for transfers between devices, exchange(): lax.all_to_all(value, axes, 0, 0, tiled=True, axis_index_groups=groups)  3.6 us
    pallas_call x1, Pallas kernels, sensitivity(): call(sensitivity_kernel, jax.ShapeDtypeStruct((SLABS, 16, 128), jnp.float...  1.69 us
  transfers between devices with their start and end apart: 5, of which 3 were waited for; matrix products, arithmetic and copies ran while one was open for 0% of the time, Pallas kernels for 1%

profile of v4, /device:TPU:1, one launch (start us, length us, event | category | flops | bytes accessed | tf_op | source)
XLA Modules:
  0.0 74.0 jit_solution(4173147837870984977)
XLA Ops:
  1.3 0.0 copy-start.2
  1.3 1.7 %shard_map.102 = f32[32,16,128]{2,1,0:T(8,128)S(1)} custom-call(bf16[1,2,3,32,16,128]{5,4,3,2,1,0:T(8,128)(2,1)} %fwd_ref.1, bf16[1,2,3,32,16,128]{5,4,3,2,1,0:T(8,128)(2,1)} %adj_ref.1, f32[1]{0:T(128)S(6)} %copy.11.weight_ref), custom_call_target="tpu_custom_call" | custom-call | tf_op jit(solution)/shard_map/pallas_call | solution.py:95
  3.0 0.0 copy-start
  3.0 0.0 copy-start.1
  3.0 24.6 %all_to_all.15.terms_ref = f32[32,16,128]{2,1,0:T(8,128)S(1)} all-to-all(f32[32,16,128]{2,1,0:T(8,128)S(1)} %shard_map.102), channel_id=1, replica_groups={{496,480,464,448,432,416,400,384,368,352,336,320,304,288,272,256,240,22..., dimensions={0} | all-to-all | bytes 524288 | tf_op jit(solution)/shard_map/all_to_all | solution.py:340
  27.6 0.0 copy-done.2
  27.6 0.0 copy-done
  27.6 0.0 copy-done.1
  27.6 0.2 shard_map.103
  27.8 0.0 copy-start.3
  27.8 14.5 %all_to_all.16.all_ref = f32[16,32,128]{2,1,0:T(8,128)S(1)} all-to-all(f32[16,32,128]{2,1,0:T(8,128)S(1)} %get-tuple-element.20), channel_id=1, replica_groups=mesh['illum'=32,'gx'=4,'gy'=4] {'gx','gy'}, dimensions={0} | all-to-all | bytes 524288 | tf_op jit(solution)/shard_map/all_to_all | solution.py:340
  42.3 0.0 copy-done.3
  42.3 1.3 %shard_map.104 = f32[32,24,128]{2,1,0:T(8,128)} custom-call(f32[16,32,128]{2,1,0:T(8,128)S(1)} %all_to_all.16.all_ref, bf16[1152,128]{1,0:T(8,128)(2,1)S(1)} %copy-done.3), custom_call_target="tpu_custom_call" | custom-call | tf_op jit(solution)/shard_map/pallas_call | solution.py:189
  43.6 9.6 %all-to-all-start.2 = ((f32[32,24,128]{2,1,0:T(8,128)}), f32[32,24,128]{2,1,0:T(8,128)S(1)}, u32[]{:S(2)}, u32[]{:S(2)}) async-start(f32[32,24,128]{2,1,0:T(8,128)} %shard_map.104), calls=%async_computation.2 | async-start | bytes 786432 | tf_op jit(solution)/shard_map/all_to_all | solution.py:340
  53.2 2.2 %collective-permute-start = (f32[3,8,16,128]{3,2,1,0:T(8,128)S(1)}, f32[3,8,16,128]{3,2,1,0:T(8,128)S(1)}, u32[]{:S(2)}, u32[]{:S(2)}) collective-permute-start(f32[3,8,16,128]{3,2,1,0:T(8,128)S(1)} %get-tuple-element.24), channel_id=1, source_target_pairs={{0,4},{4,0},{8,12},{12,8},{1,5},{5,1},{9,13},{13,9},{2,6},{6,2},{1... | collective-permute-start | bytes 589832 | tf_op jit(solution)/shard_map/ppermute | solution.py:336
  55.4 0.7 collective-permute-start.1
  56.1 4.1 %collective-permute-done.near_ref = f32[3,8,16,128]{3,2,1,0:T(8,128)S(1)} collective-permute-done((f32[3,8,16,128]{3,2,1,0:T(8,128)S(1)}, f32[3,8,16,128]{3,2,1,0:T(8,128)S(1)}, u32[]{:S(2)}, u32[]{:S(2)}) %collective-permute-start) | collective-permute-done | bytes 196640 | tf_op jit(solution)/shard_map/ppermute | solution.py:336
  60.2 0.0 collective-permute-done.1.far_ref
  60.2 3.6 %all-to-all-done.2.slabs_ref = f32[32,24,128]{2,1,0:T(8,128)S(1)} async-done(((f32[32,24,128]{2,1,0:T(8,128)}), f32[32,24,128]{2,1,0:T(8,128)S(1)}, u32[]{:S(2)}, u32[]{:S(2)}) %all-to-all-start.2) | async-done | bytes 393248 | tf_op jit(solution)/shard_map/all_to_all | solution.py:340
  63.8 0.8 %shard_map.105 = (f32[32,16,128]{2,1,0:T(8,128)S(1)}, f32[32,16,128]{2,1,0:T(8,128)S(1)}, f32[32,16,128]{2,1,0:T(8,128)S(1)}, f32[32,16,128]{2,1,0:T(8,128)S(1)}...) custom-call(f32[32,24,128]{2,1,0:T(8,128)S(1)} %all-to-all-done.2.slabs_ref, f32[32,16,128]{2,1,0:T(8,128)S(1)} %copy-done, ...), custom_call_target="tpu_custom_call" | custom-call | tf_op jit(solution)/shard_map/pallas_call | solution.py:253
  64.6 5.0 %collective-permute-start.2 = (f32[32,8,128]{2,1,0:T(8,128)S(1)}, f32[32,8,128]{2,1,0:T(8,128)S(1)}, u32[]{:S(2)}, u32[]{:S(2)}) collective-permute-start(f32[32,8,128]{2,1,0:T(8,128)S(1)} %get-tuple-element.33), channel_id=1, source_target_pairs={{1,2},{2,1},{5,6},{6,5},{9,10},{10,9},{13,14},{14,13},{17,18},{18,... | collective-permute-start | bytes 393224 | tf_op jit(solution)/shard_map/ppermute | solution.py:335
  69.7 1.9 %collective-permute-start.3 = (f32[32,8,128]{2,1,0:T(8,128)S(1)}, f32[32,8,128]{2,1,0:T(8,128)S(1)}, u32[]{:S(2)}, u32[]{:S(2)}) collective-permute-start(f32[32,8,128]{2,1,0:T(8,128)S(1)} %get-tuple-element.35), channel_id=1, source_target_pairs={{0,1},{1,0},{2,3},{3,2},{4,5},{5,4},{6,7},{7,6},{8,9},{9,8},{10,11... | collective-permute-start | bytes 393224 | tf_op jit(solution)/shard_map/ppermute | solution.py:336
  71.6 0.9 %shard_map.106 = (f32[32,16,128]{2,1,0:T(8,128)S(1)}, f32[32,16,128]{2,1,0:T(8,128)}, f32[32,16,128]{2,1,0:T(8,128)}, f32[32,16,128]{2,1,0:T(8,128)}) custom-call(f32[32,16,128]{2,1,0:T(8,128)S(1)} %get-tuple-element.26.fx_ref, f32[32,16,128]{2,1,0:T(8,128)S(1)} %get-tuple-element.27.nd_ref, f32[32,16,128]{2,1,0:T(8,128)S(1)} %get-tuple-element.28.nm_ref, ...), custom_call_target="tpu_custom_call" | custom-call | tf_op jit(solution)/shard_map/pallas_call | solution.py:291
  72.5 0.0 collective-permute-done.2.far_ref
  72.5 0.4 collective-permute-done.3.near_ref
  72.9 1.1 %shard_map.107 = f32[32,16,128]{2,1,0:T(8,128)} custom-call(f32[32,8,128]{2,1,0:T(8,128)S(1)} %collective-permute-done.2.far_ref, f32[32,16,128]{2,1,0:T(8,128)S(1)} %get-tuple-element.34.own_ref, f32[32,8,128]{2,1,0:T(8,128)S(1)} %collective-permute-done.3.near_ref), custom_call_target="tpu_custom_call" | custom-call | tf_op jit(solution)/shard_map/pallas_call | solution.py:322
Async XLA Ops:
  1.3 26.4 %copy-start.2 = (f32[32,16,128]{2,1,0:T(8,128)S(1)}, f32[32,16,128]{2,1,0:T(8,128)}, u32[]{:S(2)}) copy-start(f32[32,16,128]{2,1,0:T(8,128)} %v_ref.3) | copy-start | bytes 786436
  3.0 24.7 %copy-start = (f32[32,16,128]{2,1,0:T(8,128)S(1)}, f32[32,16,128]{2,1,0:T(8,128)}, u32[]{:S(2)}) copy-start(f32[32,16,128]{2,1,0:T(8,128)} %d_ref.3) | copy-start | bytes 786436
  3.0 24.6 %copy-start.1 = (f32[32,16,128]{2,1,0:T(8,128)S(1)}, f32[32,16,128]{2,1,0:T(8,128)}, u32[]{:S(2)}) copy-start(f32[32,16,128]{2,1,0:T(8,128)} %m_ref.3) | copy-start | bytes 786436
  27.8 14.5 %copy-start.3 = (bf16[1152,128]{1,0:T(8,128)(2,1)S(1)}, bf16[1152,128]{1,0:T(8,128)(2,1)}, u32[]{:S(2)}) copy-start(bf16[1152,128]{1,0:T(8,128)(2,1)} %constant.6.taps_ref) | copy-start | bytes 884740
  43.6 20.2 %all-to-all-start.2 = ((f32[32,24,128]{2,1,0:T(8,128)}), f32[32,24,128]{2,1,0:T(8,128)S(1)}, u32[]{:S(2)}, u32[]{:S(2)}) async-start(f32[32,24,128]{2,1,0:T(8,128)} %shard_map.104), calls=%async_computation.2 | async-start | bytes 786432 | tf_op jit(solution)/shard_map/all_to_all | solution.py:340
  53.2 7.0 %collective-permute-start = (f32[3,8,16,128]{3,2,1,0:T(8,128)S(1)}, f32[3,8,16,128]{3,2,1,0:T(8,128)S(1)}, u32[]{:S(2)}, u32[]{:S(2)}) collective-permute-start(f32[3,8,16,128]{3,2,1,0:T(8,128)S(1)} %get-tuple-element.24), channel_id=1, source_target_pairs={{0,4},{4,0},{8,12},{12,8},{1,5},{5,1},{9,13},{13,9},{2,6},{6,2},{1... | collective-permute-start | bytes 589832 | tf_op jit(solution)/shard_map/ppermute | solution.py:336
  55.4 4.8 %collective-permute-start.1 = (f32[3,8,16,128]{3,2,1,0:T(8,128)S(1)}, f32[3,8,16,128]{3,2,1,0:T(8,128)S(1)}, u32[]{:S(2)}, u32[]{:S(2)}) collective-permute-start(f32[3,8,16,128]{3,2,1,0:T(8,128)S(1)} %get-tuple-element.25), channel_id=1, source_target_pairs={{4,8},{8,4},{5,9},{9,5},{6,10},{10,6},{7,11},{11,7},{20,24},{24,20... | collective-permute-start | bytes 589832 | tf_op jit(solution)/shard_map/ppermute | solution.py:335
  64.6 7.9 %collective-permute-start.2 = (f32[32,8,128]{2,1,0:T(8,128)S(1)}, f32[32,8,128]{2,1,0:T(8,128)S(1)}, u32[]{:S(2)}, u32[]{:S(2)}) collective-permute-start(f32[32,8,128]{2,1,0:T(8,128)S(1)} %get-tuple-element.33), channel_id=1, source_target_pairs={{1,2},{2,1},{5,6},{6,5},{9,10},{10,9},{13,14},{14,13},{17,18},{18,... | collective-permute-start | bytes 393224 | tf_op jit(solution)/shard_map/ppermute | solution.py:335
  69.7 3.2 %collective-permute-start.3 = (f32[32,8,128]{2,1,0:T(8,128)S(1)}, f32[32,8,128]{2,1,0:T(8,128)S(1)}, u32[]{:S(2)}, u32[]{:S(2)}) collective-permute-start(f32[32,8,128]{2,1,0:T(8,128)S(1)} %get-tuple-element.35), channel_id=1, source_target_pairs={{0,1},{1,0},{2,3},{3,2},{4,5},{5,4},{6,7},{7,6},{8,9},{9,8},{10,11... | collective-permute-start | bytes 393224 | tf_op jit(solution)/shard_map/ppermute | solution.py:336

commit v5 on v4

--- a/solution.py
+++ b/solution.py
@@ -154,7 +154,7 @@
             for pair in range(2):
                 at = PAD_X + 4 * x + 2 * pair
                 for ref, base in ((sens, 0), (dens, 16)):
-                    tile = all_ref[4 * x + y, base + 8 * pair : base + 8 * pair + 8, :]
+                    tile = all_ref[15 - (4 * x + y), base + 8 * pair : base + 8 * pair + 8, :]
                     turned = pltpu.roll(tile, DEEP, 0)
                     twice = (jnp.where(low, tile, turned), jnp.where(low, turned, tile))
                     for odd in range(2):
@@ -340,15 +340,15 @@
     return lax.all_to_all(value, axes, 0, 0, tiled=True, axis_index_groups=groups)
 
 
-def countdown(axis):
-    return [list(reversed(range(lax.axis_size(axis))))]
+def countdown(axes):
+    return [list(reversed(range(lax.axis_size(axes))))]
 
 
 def shards(density, moment_one, moment_two, forward_field, adjoint_field, objective_weight):
     state = (density, moment_one, moment_two)
     terms = exchange(sensitivity(forward_field, adjoint_field, objective_weight), "illum", countdown("illum"))
     both, near, far = middle(terms, *state)
-    slab = slab_step(exchange(both, ("gx", "gy")))
+    slab = slab_step(exchange(both, ("gx", "gy"), countdown(("gx", "gy"))))
     slab, near, far = lax.optimization_barrier((slab, near, far))
     slabs = exchange(slab, "illum", countdown("illum"))
     near, far = swap(near, far, "gx")

time: 74.4 us -> 72.6 us (0.976)
  blocking collectives: 39.1 us -> 37.2 us
  waiting for transfers between devices: 8.14 us -> 9.13 us
  starting transfers between devices: 19.4 us -> 18.5 us
    all_to_all x2, blocking collectives: 39.1 us -> 37.2 us  [exchange(): lax.all_to_all(value, axes, 0, 0, tiled=True, axis_index_groups=groups)]
    ppermute x2, starting transfers between devices: 5.72 us -> 4.46 us  [swap(): far = lax.ppermute(far, axis, others)]
where the time goes in v5:
time: 72.6 us; the launch traced here: 72.2 us
  blocking collectives  37.2 us (51%)
  starting transfers between devices  18.5 us (25%)
  waiting for transfers between devices  9.13 us (13%)
  Pallas kernels  5.97 us (8%)
  between operations  1.39 us (2%)
    all_to_all x2, blocking collectives, exchange(): lax.all_to_all(value, axes, 0, 0, tiled=True, axis_index_groups=groups)  37.2 us
    all_to_all x1, starting transfers between devices, exchange(): lax.all_to_all(value, axes, 0, 0, tiled=True, axis_index_groups=groups)  9.56 us
    ppermute x2, waiting for transfers between devices, swap(): return (lax.ppermute(near, axis, pairs), far)  5.1 us
    ppermute x2, starting transfers between devices, swap(): return (lax.ppermute(near, axis, pairs), far)  4.47 us
    ppermute x2, starting transfers between devices, swap(): far = lax.ppermute(far, axis, others)  4.46 us
    all_to_all x1, waiting for transfers between devices, exchange(): lax.all_to_all(value, axes, 0, 0, tiled=True, axis_index_groups=groups)  4.02 us
    pallas_call x1, Pallas kernels, sensitivity(): call(sensitivity_kernel, jax.ShapeDtypeStruct((SLABS, 16, 128), jnp.float...  1.69 us
  transfers between devices with their start and end apart: 5, of which 3 were waited for; matrix products, arithmetic and copies ran while one was open for 0% of the time, Pallas kernels for 1%

profile of v5, /device:TPU:1, one launch (start us, length us, event | category | flops | bytes accessed | tf_op | source)
XLA Modules:
  0.0 72.2 jit_solution(14067555060154513879)
XLA Ops:
  1.3 0.0 copy-start.2
  1.3 1.7 %shard_map.102 = f32[32,16,128]{2,1,0:T(8,128)S(1)} custom-call(bf16[1,2,3,32,16,128]{5,4,3,2,1,0:T(8,128)(2,1)} %fwd_ref.1, bf16[1,2,3,32,16,128]{5,4,3,2,1,0:T(8,128)(2,1)} %adj_ref.1, f32[1]{0:T(128)S(6)} %copy.11.weight_ref), custom_call_target="tpu_custom_call" | custom-call | tf_op jit(solution)/shard_map/pallas_call | solution.py:95
  3.0 0.0 copy-start
  3.0 0.0 copy-start.1
  3.0 24.6 %all_to_all.15.terms_ref = f32[32,16,128]{2,1,0:T(8,128)S(1)} all-to-all(f32[32,16,128]{2,1,0:T(8,128)S(1)} %shard_map.102), channel_id=1, replica_groups={{496,480,464,448,432,416,400,384,368,352,336,320,304,288,272,256,240,22..., dimensions={0} | all-to-all | bytes 524288 | tf_op jit(solution)/shard_map/all_to_all | solution.py:340
  27.6 0.0 copy-done.2
  27.6 0.0 copy-done
  27.6 0.0 copy-done.1
  27.6 0.2 shard_map.103
  27.8 0.0 copy-start.3
  27.8 12.6 %all_to_all.16.all_ref = f32[16,32,128]{2,1,0:T(8,128)S(1)} all-to-all(f32[16,32,128]{2,1,0:T(8,128)S(1)} %get-tuple-element.20), channel_id=1, replica_groups={{15,14,13,12,11,10,9,8,7,6,5,4,3,2,1,0},{31,30,29,28,27,26,25,24,23,22,..., dimensions={0} | all-to-all | bytes 524288 | tf_op jit(solution)/shard_map/all_to_all | solution.py:340
  40.4 0.0 copy-done.3
  40.4 1.3 %shard_map.104 = f32[32,24,128]{2,1,0:T(8,128)} custom-call(f32[16,32,128]{2,1,0:T(8,128)S(1)} %all_to_all.16.all_ref, bf16[1152,128]{1,0:T(8,128)(2,1)S(1)} %copy-done.3), custom_call_target="tpu_custom_call" | custom-call | tf_op jit(solution)/shard_map/pallas_call | solution.py:189
  41.7 9.6 %all-to-all-start.2 = ((f32[32,24,128]{2,1,0:T(8,128)}), f32[32,24,128]{2,1,0:T(8,128)S(1)}, u32[]{:S(2)}, u32[]{:S(2)}) async-start(f32[32,24,128]{2,1,0:T(8,128)} %shard_map.104), calls=%async_computation.2 | async-start | bytes 786432 | tf_op jit(solution)/shard_map/all_to_all | solution.py:340
  51.3 2.5 %collective-permute-start = (f32[3,8,16,128]{3,2,1,0:T(8,128)S(1)}, f32[3,8,16,128]{3,2,1,0:T(8,128)S(1)}, u32[]{:S(2)}, u32[]{:S(2)}) collective-permute-start(f32[3,8,16,128]{3,2,1,0:T(8,128)S(1)} %get-tuple-element.24), channel_id=1, source_target_pairs={{0,4},{4,0},{8,12},{12,8},{1,5},{5,1},{9,13},{13,9},{2,6},{6,2},{1... | collective-permute-start | bytes 589832 | tf_op jit(solution)/shard_map/ppermute | solution.py:336
  53.9 0.7 collective-permute-start.1
  54.5 4.7 %collective-permute-done.near_ref = f32[3,8,16,128]{3,2,1,0:T(8,128)S(1)} collective-permute-done((f32[3,8,16,128]{3,2,1,0:T(8,128)S(1)}, f32[3,8,16,128]{3,2,1,0:T(8,128)S(1)}, u32[]{:S(2)}, u32[]{:S(2)}) %collective-permute-start) | collective-permute-done | bytes 196640 | tf_op jit(solution)/shard_map/ppermute | solution.py:336
  59.2 0.0 collective-permute-done.1.far_ref
  59.2 4.0 %all-to-all-done.2.slabs_ref = f32[32,24,128]{2,1,0:T(8,128)S(1)} async-done(((f32[32,24,128]{2,1,0:T(8,128)}), f32[32,24,128]{2,1,0:T(8,128)S(1)}, u32[]{:S(2)}, u32[]{:S(2)}) %all-to-all-start.2) | async-done | bytes 393248 | tf_op jit(solution)/shard_map/all_to_all | solution.py:340
  63.3 0.8 %shard_map.105 = (f32[32,16,128]{2,1,0:T(8,128)S(1)}, f32[32,16,128]{2,1,0:T(8,128)S(1)}, f32[32,16,128]{2,1,0:T(8,128)S(1)}, f32[32,16,128]{2,1,0:T(8,128)S(1)}...) custom-call(f32[32,24,128]{2,1,0:T(8,128)S(1)} %all-to-all-done.2.slabs_ref, f32[32,16,128]{2,1,0:T(8,128)S(1)} %copy-done, ...), custom_call_target="tpu_custom_call" | custom-call | tf_op jit(solution)/shard_map/pallas_call | solution.py:253
  64.0 3.8 %collective-permute-start.2 = (f32[32,8,128]{2,1,0:T(8,128)S(1)}, f32[32,8,128]{2,1,0:T(8,128)S(1)}, u32[]{:S(2)}, u32[]{:S(2)}) collective-permute-start(f32[32,8,128]{2,1,0:T(8,128)S(1)} %get-tuple-element.33), channel_id=1, source_target_pairs={{1,2},{2,1},{5,6},{6,5},{9,10},{10,9},{13,14},{14,13},{17,18},{18,... | collective-permute-start | bytes 393224 | tf_op jit(solution)/shard_map/ppermute | solution.py:335
  67.8 1.9 %collective-permute-start.3 = (f32[32,8,128]{2,1,0:T(8,128)S(1)}, f32[32,8,128]{2,1,0:T(8,128)S(1)}, u32[]{:S(2)}, u32[]{:S(2)}) collective-permute-start(f32[32,8,128]{2,1,0:T(8,128)S(1)} %get-tuple-element.35), channel_id=1, source_target_pairs={{0,1},{1,0},{2,3},{3,2},{4,5},{5,4},{6,7},{7,6},{8,9},{9,8},{10,11... | collective-permute-start | bytes 393224 | tf_op jit(solution)/shard_map/ppermute | solution.py:336
  69.8 0.9 %shard_map.106 = (f32[32,16,128]{2,1,0:T(8,128)S(1)}, f32[32,16,128]{2,1,0:T(8,128)}, f32[32,16,128]{2,1,0:T(8,128)}, f32[32,16,128]{2,1,0:T(8,128)}) custom-call(f32[32,16,128]{2,1,0:T(8,128)S(1)} %get-tuple-element.26.fx_ref, f32[32,16,128]{2,1,0:T(8,128)S(1)} %get-tuple-element.27.nd_ref, f32[32,16,128]{2,1,0:T(8,128)S(1)} %get-tuple-element.28.nm_ref, ...), custom_call_target="tpu_custom_call" | custom-call | tf_op jit(solution)/shard_map/pallas_call | solution.py:291
  70.7 0.0 collective-permute-done.2.far_ref
  70.7 0.4 collective-permute-done.3.near_ref
  71.1 1.1 %shard_map.107 = f32[32,16,128]{2,1,0:T(8,128)} custom-call(f32[32,8,128]{2,1,0:T(8,128)S(1)} %collective-permute-done.2.far_ref, f32[32,16,128]{2,1,0:T(8,128)S(1)} %get-tuple-element.34.own_ref, f32[32,8,128]{2,1,0:T(8,128)S(1)} %collective-permute-done.3.near_ref), custom_call_target="tpu_custom_call" | custom-call | tf_op jit(solution)/shard_map/pallas_call | solution.py:322
Async XLA Ops:
  1.3 26.4 %copy-start.2 = (f32[32,16,128]{2,1,0:T(8,128)S(1)}, f32[32,16,128]{2,1,0:T(8,128)}, u32[]{:S(2)}) copy-start(f32[32,16,128]{2,1,0:T(8,128)} %v_ref.3) | copy-start | bytes 786436
  3.0 24.7 %copy-start = (f32[32,16,128]{2,1,0:T(8,128)S(1)}, f32[32,16,128]{2,1,0:T(8,128)}, u32[]{:S(2)}) copy-start(f32[32,16,128]{2,1,0:T(8,128)} %d_ref.3) | copy-start | bytes 786436
  3.0 24.6 %copy-start.1 = (f32[32,16,128]{2,1,0:T(8,128)S(1)}, f32[32,16,128]{2,1,0:T(8,128)}, u32[]{:S(2)}) copy-start(f32[32,16,128]{2,1,0:T(8,128)} %m_ref.3) | copy-start | bytes 786436
  27.8 12.6 %copy-start.3 = (bf16[1152,128]{1,0:T(8,128)(2,1)S(1)}, bf16[1152,128]{1,0:T(8,128)(2,1)}, u32[]{:S(2)}) copy-start(bf16[1152,128]{1,0:T(8,128)(2,1)} %constant.6.taps_ref) | copy-start | bytes 884740
  41.7 21.5 %all-to-all-start.2 = ((f32[32,24,128]{2,1,0:T(8,128)}), f32[32,24,128]{2,1,0:T(8,128)S(1)}, u32[]{:S(2)}, u32[]{:S(2)}) async-start(f32[32,24,128]{2,1,0:T(8,128)} %shard_map.104), calls=%async_computation.2 | async-start | bytes 786432 | tf_op jit(solution)/shard_map/all_to_all | solution.py:340
  51.3 7.9 %collective-permute-start = (f32[3,8,16,128]{3,2,1,0:T(8,128)S(1)}, f32[3,8,16,128]{3,2,1,0:T(8,128)S(1)}, u32[]{:S(2)}, u32[]{:S(2)}) collective-permute-start(f32[3,8,16,128]{3,2,1,0:T(8,128)S(1)} %get-tuple-element.24), channel_id=1, source_target_pairs={{0,4},{4,0},{8,12},{12,8},{1,5},{5,1},{9,13},{13,9},{2,6},{6,2},{1... | collective-permute-start | bytes 589832 | tf_op jit(solution)/shard_map/ppermute | solution.py:336
  53.9 5.4 %collective-permute-start.1 = (f32[3,8,16,128]{3,2,1,0:T(8,128)S(1)}, f32[3,8,16,128]{3,2,1,0:T(8,128)S(1)}, u32[]{:S(2)}, u32[]{:S(2)}) collective-permute-start(f32[3,8,16,128]{3,2,1,0:T(8,128)S(1)} %get-tuple-element.25), channel_id=1, source_target_pairs={{4,8},{8,4},{5,9},{9,5},{6,10},{10,6},{7,11},{11,7},{20,24},{24,20... | collective-permute-start | bytes 589832 | tf_op jit(solution)/shard_map/ppermute | solution.py:335
  64.0 6.6 %collective-permute-start.2 = (f32[32,8,128]{2,1,0:T(8,128)S(1)}, f32[32,8,128]{2,1,0:T(8,128)S(1)}, u32[]{:S(2)}, u32[]{:S(2)}) collective-permute-start(f32[32,8,128]{2,1,0:T(8,128)S(1)} %get-tuple-element.33), channel_id=1, source_target_pairs={{1,2},{2,1},{5,6},{6,5},{9,10},{10,9},{13,14},{14,13},{17,18},{18,... | collective-permute-start | bytes 393224 | tf_op jit(solution)/shard_map/ppermute | solution.py:335
  67.8 3.2 %collective-permute-start.3 = (f32[32,8,128]{2,1,0:T(8,128)S(1)}, f32[32,8,128]{2,1,0:T(8,128)S(1)}, u32[]{:S(2)}, u32[]{:S(2)}) collective-permute-start(f32[32,8,128]{2,1,0:T(8,128)S(1)} %get-tuple-element.35), channel_id=1, source_target_pairs={{0,1},{1,0},{2,3},{3,2},{4,5},{5,4},{6,7},{7,6},{8,9},{9,8},{10,11... | collective-permute-start | bytes 393224 | tf_op jit(solution)/shard_map/ppermute | solution.py:336

commit v6 on v5

--- a/solution.py
+++ b/solution.py
@@ -154,7 +154,7 @@
             for pair in range(2):
                 at = PAD_X + 4 * x + 2 * pair
                 for ref, base in ((sens, 0), (dens, 16)):
-                    tile = all_ref[15 - (4 * x + y), base + 8 * pair : base + 8 * pair + 8, :]
+                    tile = all_ref[15 - (4 * y + x), base + 8 * pair : base + 8 * pair + 8, :]
                     turned = pltpu.roll(tile, DEEP, 0)
                     twice = (jnp.where(low, tile, turned), jnp.where(low, turned, tile))
                     for odd in range(2):
@@ -348,7 +348,7 @@
     state = (density, moment_one, moment_two)
     terms = exchange(sensitivity(forward_field, adjoint_field, objective_weight), "illum", countdown("illum"))
     both, near, far = middle(terms, *state)
-    slab = slab_step(exchange(both, ("gx", "gy"), countdown(("gx", "gy"))))
+    slab = slab_step(exchange(both, ("gy", "gx"), countdown(("gy", "gx"))))
     slab, near, far = lax.optimization_barrier((slab, near, far))
     slabs = exchange(slab, "illum", countdown("illum"))
     near, far = swap(near, far, "gx")

time: 72.6 us -> 72.3 us (level)
  waiting for transfers between devices: 9.13 us -> 7.75 us
  starting transfers between devices: 18.5 us -> 19.7 us
    ppermute x2, starting transfers between devices: 4.46 us -> 5.83 us  [swap(): far = lax.ppermute(far, axis, others)]
    ppermute x2, waiting for transfers between devices: 5.1 us -> 4.13 us  [swap(): return (lax.ppermute(near, axis, pairs), far)]
where the time goes in v6:
time: 72.3 us; the launch traced here: 71.9 us
  blocking collectives  37.1 us (51%)
  starting transfers between devices  19.7 us (27%)
  waiting for transfers between devices  7.75 us (11%)
  Pallas kernels  5.98 us (8%)
  between operations  1.39 us (2%)
    all_to_all x2, blocking collectives, exchange(): lax.all_to_all(value, axes, 0, 0, tiled=True, axis_index_groups=groups)  37.1 us
    all_to_all x1, starting transfers between devices, exchange(): lax.all_to_all(value, axes, 0, 0, tiled=True, axis_index_groups=groups)  9.56 us
    ppermute x2, starting transfers between devices, swap(): far = lax.ppermute(far, axis, others)  5.83 us
    ppermute x2, starting transfers between devices, swap(): return (lax.ppermute(near, axis, pairs), far)  4.33 us
    ppermute x2, waiting for transfers between devices, swap(): return (lax.ppermute(near, axis, pairs), far)  4.13 us
    all_to_all x1, waiting for transfers between devices, exchange(): lax.all_to_all(value, axes, 0, 0, tiled=True, axis_index_groups=groups)  3.62 us
    pallas_call x1, Pallas kernels, sensitivity(): call(sensitivity_kernel, jax.ShapeDtypeStruct((SLABS, 16, 128), jnp.float...  1.69 us
  transfers between devices with their start and end apart: 5, of which 3 were waited for; matrix products, arithmetic and copies ran while one was open for 0% of the time, Pallas kernels for 1%

profile of v6, /device:TPU:1, one launch (start us, length us, event | category | flops | bytes accessed | tf_op | source)
XLA Modules:
  0.0 71.9 jit_solution(13774504231994948645)
XLA Ops:
  1.3 0.0 copy-start.2
  1.3 1.7 %shard_map.102 = f32[32,16,128]{2,1,0:T(8,128)S(1)} custom-call(bf16[1,2,3,32,16,128]{5,4,3,2,1,0:T(8,128)(2,1)} %fwd_ref.1, bf16[1,2,3,32,16,128]{5,4,3,2,1,0:T(8,128)(2,1)} %adj_ref.1, f32[1]{0:T(128)S(6)} %copy.11.weight_ref), custom_call_target="tpu_custom_call" | custom-call | tf_op jit(solution)/shard_map/pallas_call | solution.py:95
  3.0 0.0 copy-start
  3.0 0.0 copy-start.1
  3.0 24.6 %all_to_all.15.terms_ref = f32[32,16,128]{2,1,0:T(8,128)S(1)} all-to-all(f32[32,16,128]{2,1,0:T(8,128)S(1)} %shard_map.102), channel_id=1, replica_groups={{496,480,464,448,432,416,400,384,368,352,336,320,304,288,272,256,240,22..., dimensions={0} | all-to-all | bytes 524288 | tf_op jit(solution)/shard_map/all_to_all | solution.py:340
  27.6 0.0 copy-done.2
  27.6 0.0 copy-done
  27.6 0.0 copy-done.1
  27.6 0.2 shard_map.103
  27.8 0.0 copy-start.3
  27.8 12.4 %all_to_all.16.all_ref = f32[16,32,128]{2,1,0:T(8,128)S(1)} all-to-all(f32[16,32,128]{2,1,0:T(8,128)S(1)} %get-tuple-element.20), channel_id=1, replica_groups={{15,11,7,3,14,10,6,2,13,9,5,1,12,8,4,0},{31,27,23,19,30,26,22,18,29,25,..., dimensions={0} | all-to-all | bytes 524288 | tf_op jit(solution)/shard_map/all_to_all | solution.py:340
  40.3 0.0 copy-done.3
  40.3 1.3 %shard_map.104 = f32[32,24,128]{2,1,0:T(8,128)} custom-call(f32[16,32,128]{2,1,0:T(8,128)S(1)} %all_to_all.16.all_ref, bf16[1152,128]{1,0:T(8,128)(2,1)S(1)} %copy-done.3), custom_call_target="tpu_custom_call" | custom-call | tf_op jit(solution)/shard_map/pallas_call | solution.py:189
  41.6 9.6 %all-to-all-start.2 = ((f32[32,24,128]{2,1,0:T(8,128)}), f32[32,24,128]{2,1,0:T(8,128)S(1)}, u32[]{:S(2)}, u32[]{:S(2)}) async-start(f32[32,24,128]{2,1,0:T(8,128)} %shard_map.104), calls=%async_computation.2 | async-start | bytes 786432 | tf_op jit(solution)/shard_map/all_to_all | solution.py:340
  51.2 2.4 %collective-permute-start = (f32[3,8,16,128]{3,2,1,0:T(8,128)S(1)}, f32[3,8,16,128]{3,2,1,0:T(8,128)S(1)}, u32[]{:S(2)}, u32[]{:S(2)}) collective-permute-start(f32[3,8,16,128]{3,2,1,0:T(8,128)S(1)} %get-tuple-element.24), channel_id=1, source_target_pairs={{0,4},{4,0},{8,12},{12,8},{1,5},{5,1},{9,13},{13,9},{2,6},{6,2},{1... | collective-permute-start | bytes 589832 | tf_op jit(solution)/shard_map/ppermute | solution.py:336
  53.6 0.7 collective-permute-start.1
  54.3 3.7 %collective-permute-done.near_ref = f32[3,8,16,128]{3,2,1,0:T(8,128)S(1)} collective-permute-done((f32[3,8,16,128]{3,2,1,0:T(8,128)S(1)}, f32[3,8,16,128]{3,2,1,0:T(8,128)S(1)}, u32[]{:S(2)}, u32[]{:S(2)}) %collective-permute-start) | collective-permute-done | bytes 196640 | tf_op jit(solution)/shard_map/ppermute | solution.py:336
  58.0 0.0 collective-permute-done.1.far_ref
  58.0 3.6 %all-to-all-done.2.slabs_ref = f32[32,24,128]{2,1,0:T(8,128)S(1)} async-done(((f32[32,24,128]{2,1,0:T(8,128)}), f32[32,24,128]{2,1,0:T(8,128)S(1)}, u32[]{:S(2)}, u32[]{:S(2)}) %all-to-all-start.2) | async-done | bytes 393248 | tf_op jit(solution)/shard_map/all_to_all | solution.py:340
  61.6 0.8 %shard_map.105 = (f32[32,16,128]{2,1,0:T(8,128)S(1)}, f32[32,16,128]{2,1,0:T(8,128)S(1)}, f32[32,16,128]{2,1,0:T(8,128)S(1)}, f32[32,16,128]{2,1,0:T(8,128)S(1)}...) custom-call(f32[32,24,128]{2,1,0:T(8,128)S(1)} %all-to-all-done.2.slabs_ref, f32[32,16,128]{2,1,0:T(8,128)S(1)} %copy-done, ...), custom_call_target="tpu_custom_call" | custom-call | tf_op jit(solution)/shard_map/pallas_call | solution.py:253
  62.4 5.2 %collective-permute-start.2 = (f32[32,8,128]{2,1,0:T(8,128)S(1)}, f32[32,8,128]{2,1,0:T(8,128)S(1)}, u32[]{:S(2)}, u32[]{:S(2)}) collective-permute-start(f32[32,8,128]{2,1,0:T(8,128)S(1)} %get-tuple-element.33), channel_id=1, source_target_pairs={{1,2},{2,1},{5,6},{6,5},{9,10},{10,9},{13,14},{14,13},{17,18},{18,... | collective-permute-start | bytes 393224 | tf_op jit(solution)/shard_map/ppermute | solution.py:335
  67.6 1.9 %collective-permute-start.3 = (f32[32,8,128]{2,1,0:T(8,128)S(1)}, f32[32,8,128]{2,1,0:T(8,128)S(1)}, u32[]{:S(2)}, u32[]{:S(2)}) collective-permute-start(f32[32,8,128]{2,1,0:T(8,128)S(1)} %get-tuple-element.35), channel_id=1, source_target_pairs={{0,1},{1,0},{2,3},{3,2},{4,5},{5,4},{6,7},{7,6},{8,9},{9,8},{10,11... | collective-permute-start | bytes 393224 | tf_op jit(solution)/shard_map/ppermute | solution.py:336
  69.5 0.9 %shard_map.106 = (f32[32,16,128]{2,1,0:T(8,128)S(1)}, f32[32,16,128]{2,1,0:T(8,128)}, f32[32,16,128]{2,1,0:T(8,128)}, f32[32,16,128]{2,1,0:T(8,128)}) custom-call(f32[32,16,128]{2,1,0:T(8,128)S(1)} %get-tuple-element.26.fx_ref, f32[32,16,128]{2,1,0:T(8,128)S(1)} %get-tuple-element.27.nd_ref, f32[32,16,128]{2,1,0:T(8,128)S(1)} %get-tuple-element.28.nm_ref, ...), custom_call_target="tpu_custom_call" | custom-call | tf_op jit(solution)/shard_map/pallas_call | solution.py:291
  70.4 0.0 collective-permute-done.2.far_ref
  70.4 0.4 collective-permute-done.3.near_ref
  70.8 1.1 %shard_map.107 = f32[32,16,128]{2,1,0:T(8,128)} custom-call(f32[32,8,128]{2,1,0:T(8,128)S(1)} %collective-permute-done.2.far_ref, f32[32,16,128]{2,1,0:T(8,128)S(1)} %get-tuple-element.34.own_ref, f32[32,8,128]{2,1,0:T(8,128)S(1)} %collective-permute-done.3.near_ref), custom_call_target="tpu_custom_call" | custom-call | tf_op jit(solution)/shard_map/pallas_call | solution.py:322
Async XLA Ops:
  1.3 26.4 %copy-start.2 = (f32[32,16,128]{2,1,0:T(8,128)S(1)}, f32[32,16,128]{2,1,0:T(8,128)}, u32[]{:S(2)}) copy-start(f32[32,16,128]{2,1,0:T(8,128)} %v_ref.3) | copy-start | bytes 786436
  3.0 24.7 %copy-start = (f32[32,16,128]{2,1,0:T(8,128)S(1)}, f32[32,16,128]{2,1,0:T(8,128)}, u32[]{:S(2)}) copy-start(f32[32,16,128]{2,1,0:T(8,128)} %d_ref.3) | copy-start | bytes 786436
  3.0 24.6 %copy-start.1 = (f32[32,16,128]{2,1,0:T(8,128)S(1)}, f32[32,16,128]{2,1,0:T(8,128)}, u32[]{:S(2)}) copy-start(f32[32,16,128]{2,1,0:T(8,128)} %m_ref.3) | copy-start | bytes 786436
  27.8 12.5 %copy-start.3 = (bf16[1152,128]{1,0:T(8,128)(2,1)S(1)}, bf16[1152,128]{1,0:T(8,128)(2,1)}, u32[]{:S(2)}) copy-start(bf16[1152,128]{1,0:T(8,128)(2,1)} %constant.6.taps_ref) | copy-start | bytes 884740
  41.6 20.0 %all-to-all-start.2 = ((f32[32,24,128]{2,1,0:T(8,128)}), f32[32,24,128]{2,1,0:T(8,128)S(1)}, u32[]{:S(2)}, u32[]{:S(2)}) async-start(f32[32,24,128]{2,1,0:T(8,128)} %shard_map.104), calls=%async_computation.2 | async-start | bytes 786432 | tf_op jit(solution)/shard_map/all_to_all | solution.py:340
  51.2 6.8 %collective-permute-start = (f32[3,8,16,128]{3,2,1,0:T(8,128)S(1)}, f32[3,8,16,128]{3,2,1,0:T(8,128)S(1)}, u32[]{:S(2)}, u32[]{:S(2)}) collective-permute-start(f32[3,8,16,128]{3,2,1,0:T(8,128)S(1)} %get-tuple-element.24), channel_id=1, source_target_pairs={{0,4},{4,0},{8,12},{12,8},{1,5},{5,1},{9,13},{13,9},{2,6},{6,2},{1... | collective-permute-start | bytes 589832 | tf_op jit(solution)/shard_map/ppermute | solution.py:336
  53.6 4.4 %collective-permute-start.1 = (f32[3,8,16,128]{3,2,1,0:T(8,128)S(1)}, f32[3,8,16,128]{3,2,1,0:T(8,128)S(1)}, u32[]{:S(2)}, u32[]{:S(2)}) collective-permute-start(f32[3,8,16,128]{3,2,1,0:T(8,128)S(1)} %get-tuple-element.25), channel_id=1, source_target_pairs={{4,8},{8,4},{5,9},{9,5},{6,10},{10,6},{7,11},{11,7},{20,24},{24,20... | collective-permute-start | bytes 589832 | tf_op jit(solution)/shard_map/ppermute | solution.py:335
  62.4 8.0 %collective-permute-start.2 = (f32[32,8,128]{2,1,0:T(8,128)S(1)}, f32[32,8,128]{2,1,0:T(8,128)S(1)}, u32[]{:S(2)}, u32[]{:S(2)}) collective-permute-start(f32[32,8,128]{2,1,0:T(8,128)S(1)} %get-tuple-element.33), channel_id=1, source_target_pairs={{1,2},{2,1},{5,6},{6,5},{9,10},{10,9},{13,14},{14,13},{17,18},{18,... | collective-permute-start | bytes 393224 | tf_op jit(solution)/shard_map/ppermute | solution.py:335
  67.6 3.2 %collective-permute-start.3 = (f32[32,8,128]{2,1,0:T(8,128)S(1)}, f32[32,8,128]{2,1,0:T(8,128)S(1)}, u32[]{:S(2)}, u32[]{:S(2)}) collective-permute-start(f32[32,8,128]{2,1,0:T(8,128)S(1)} %get-tuple-element.35), channel_id=1, source_target_pairs={{0,1},{1,0},{2,3},{3,2},{4,5},{5,4},{6,7},{7,6},{8,9},{9,8},{10,11... | collective-permute-start | bytes 393224 | tf_op jit(solution)/shard_map/ppermute | solution.py:336

commit v7 on v6

--- a/solution.py
+++ b/solution.py
@@ -216,7 +216,7 @@
     gx, gy = lax.axis_index("gx"), lax.axis_index("gy")
     even_x, even_y = (gx & 1) == 0, (gy & 1) == 0
     rows, cols = iota((256, 256), 0), iota((256, 256), 1)
-    depth = (rows >> 3) * DEEP + (rows & 3)
+    depth = (SLABS - 1 - (rows >> 3)) * DEEP + (rows & 3)
     near = jnp.where(((rows >> 2) & 1) == (cols >> 7), hat(depth, cols & 127), 0)
     band = bf(near.astype(jnp.float32))
     for pair in range(3):
@@ -350,7 +350,7 @@
     both, near, far = middle(terms, *state)
     slab = slab_step(exchange(both, ("gy", "gx"), countdown(("gy", "gx"))))
     slab, near, far = lax.optimization_barrier((slab, near, far))
-    slabs = exchange(slab, "illum", countdown("illum"))
+    slabs = exchange(slab, "illum")
     near, far = swap(near, far, "gx")
     *results, along_x, near, far = adam_step(slabs, *state, near, far)
     near, far = swap(near, far, "gy")

time: 72.3 us -> 76.7 us (1.061)
  waiting for transfers between devices: 7.75 us -> 11 us
  starting transfers between devices: 19.7 us -> 20.9 us
    all_to_all x1, waiting for transfers between devices: 3.62 us -> 6.81 us  [exchange(): lax.all_to_all(value, axes, 0, 0, tiled=True, axis_index_groups=groups)]
    ppermute x2, starting transfers between devices: 5.83 us -> 7.6 us  [swap(): far = lax.ppermute(far, axis, others)]
where the time goes in v7:
time: 76.7 us; the launch traced here: 76.4 us
  blocking collectives  37.1 us (48%)
  starting transfers between devices  20.9 us (27%)
  waiting for transfers between devices  11 us (14%)
  Pallas kernels  5.99 us (8%)
  between operations  1.39 us (2%)
    all_to_all x2, blocking collectives, exchange(): lax.all_to_all(value, axes, 0, 0, tiled=True, axis_index_groups=groups)  37.1 us
    all_to_all x1, starting transfers between devices, exchange(): lax.all_to_all(value, axes, 0, 0, tiled=True, axis_index_groups=groups)  9.01 us
    ppermute x2, starting transfers between devices, swap(): far = lax.ppermute(far, axis, others)  7.6 us
    all_to_all x1, waiting for transfers between devices, exchange(): lax.all_to_all(value, axes, 0, 0, tiled=True, axis_index_groups=groups)  6.81 us
    ppermute x2, starting transfers between devices, swap(): return (lax.ppermute(near, axis, pairs), far)  4.32 us
    ppermute x2, waiting for transfers between devices, swap(): return (lax.ppermute(near, axis, pairs), far)  4.15 us
    pallas_call x1, Pallas kernels, sensitivity(): call(sensitivity_kernel, jax.ShapeDtypeStruct((SLABS, 16, 128), jnp.float...  1.69 us
  transfers between devices with their start and end apart: 5, of which 3 were waited for; matrix products, arithmetic and copies ran while one was open for 0% of the time, Pallas kernels for 1%

profile of v7, /device:TPU:1, one launch (start us, length us, event | category | flops | bytes accessed | tf_op | source)
XLA Modules:
  0.0 76.4 jit_solution(6590311153485975190)
XLA Ops:
  1.3 0.0 copy-start.2
  1.3 1.7 %shard_map.102 = f32[32,16,128]{2,1,0:T(8,128)S(1)} custom-call(bf16[1,2,3,32,16,128]{5,4,3,2,1,0:T(8,128)(2,1)} %fwd_ref.1, bf16[1,2,3,32,16,128]{5,4,3,2,1,0:T(8,128)(2,1)} %adj_ref.1, f32[1]{0:T(128)S(6)} %copy.11.weight_ref), custom_call_target="tpu_custom_call" | custom-call | tf_op jit(solution)/shard_map/pallas_call | solution.py:95
  3.0 0.0 copy-start
  3.0 0.0 copy-start.1
  3.0 24.6 %all_to_all.15.terms_ref = f32[32,16,128]{2,1,0:T(8,128)S(1)} all-to-all(f32[32,16,128]{2,1,0:T(8,128)S(1)} %shard_map.102), channel_id=1, replica_groups={{496,480,464,448,432,416,400,384,368,352,336,320,304,288,272,256,240,22..., dimensions={0} | all-to-all | bytes 524288 | tf_op jit(solution)/shard_map/all_to_all | solution.py:340
  27.6 0.0 copy-done.2
  27.6 0.0 copy-done
  27.6 0.0 copy-done.1
  27.6 0.2 shard_map.103
  27.8 0.0 copy-start.3
  27.8 12.4 %all_to_all.16.all_ref = f32[16,32,128]{2,1,0:T(8,128)S(1)} all-to-all(f32[16,32,128]{2,1,0:T(8,128)S(1)} %get-tuple-element.20), channel_id=1, replica_groups={{15,11,7,3,14,10,6,2,13,9,5,1,12,8,4,0},{31,27,23,19,30,26,22,18,29,25,..., dimensions={0} | all-to-all | bytes 524288 | tf_op jit(solution)/shard_map/all_to_all | solution.py:340
  40.3 0.0 copy-done.3
  40.3 1.3 %shard_map.104 = f32[32,24,128]{2,1,0:T(8,128)} custom-call(f32[16,32,128]{2,1,0:T(8,128)S(1)} %all_to_all.16.all_ref, bf16[1152,128]{1,0:T(8,128)(2,1)S(1)} %copy-done.3), custom_call_target="tpu_custom_call" | custom-call | tf_op jit(solution)/shard_map/pallas_call | solution.py:189
  41.6 9.0 %all-to-all-start.2 = ((f32[32,24,128]{2,1,0:T(8,128)}), f32[32,24,128]{2,1,0:T(8,128)S(1)}, u32[]{:S(2)}, u32[]{:S(2)}) async-start(f32[32,24,128]{2,1,0:T(8,128)} %shard_map.104), calls=%async_computation.2 | async-start | bytes 786432 | tf_op jit(solution)/shard_map/all_to_all | solution.py:340
  50.6 2.4 %collective-permute-start = (f32[3,8,16,128]{3,2,1,0:T(8,128)S(1)}, f32[3,8,16,128]{3,2,1,0:T(8,128)S(1)}, u32[]{:S(2)}, u32[]{:S(2)}) collective-permute-start(f32[3,8,16,128]{3,2,1,0:T(8,128)S(1)} %get-tuple-element.24), channel_id=1, source_target_pairs={{0,4},{4,0},{8,12},{12,8},{1,5},{5,1},{9,13},{13,9},{2,6},{6,2},{1... | collective-permute-start | bytes 589832 | tf_op jit(solution)/shard_map/ppermute | solution.py:336
  53.0 0.7 collective-permute-start.1
  53.7 3.8 %collective-permute-done.near_ref = f32[3,8,16,128]{3,2,1,0:T(8,128)S(1)} collective-permute-done((f32[3,8,16,128]{3,2,1,0:T(8,128)S(1)}, f32[3,8,16,128]{3,2,1,0:T(8,128)S(1)}, u32[]{:S(2)}, u32[]{:S(2)}) %collective-permute-start) | collective-permute-done | bytes 196640 | tf_op jit(solution)/shard_map/ppermute | solution.py:336
  57.5 0.0 collective-permute-done.1.far_ref
  57.5 6.8 %all-to-all-done.2.slabs_ref = f32[32,24,128]{2,1,0:T(8,128)S(1)} async-done(((f32[32,24,128]{2,1,0:T(8,128)}), f32[32,24,128]{2,1,0:T(8,128)S(1)}, u32[]{:S(2)}, u32[]{:S(2)}) %all-to-all-start.2) | async-done | bytes 393248 | tf_op jit(solution)/shard_map/all_to_all | solution.py:340
  64.3 0.8 %shard_map.105 = (f32[32,16,128]{2,1,0:T(8,128)S(1)}, f32[32,16,128]{2,1,0:T(8,128)S(1)}, f32[32,16,128]{2,1,0:T(8,128)S(1)}, f32[32,16,128]{2,1,0:T(8,128)S(1)}...) custom-call(f32[32,24,128]{2,1,0:T(8,128)S(1)} %all-to-all-done.2.slabs_ref, f32[32,16,128]{2,1,0:T(8,128)S(1)} %copy-done, ...), custom_call_target="tpu_custom_call" | custom-call | tf_op jit(solution)/shard_map/pallas_call | solution.py:253
  65.1 6.9 %collective-permute-start.2 = (f32[32,8,128]{2,1,0:T(8,128)S(1)}, f32[32,8,128]{2,1,0:T(8,128)S(1)}, u32[]{:S(2)}, u32[]{:S(2)}) collective-permute-start(f32[32,8,128]{2,1,0:T(8,128)S(1)} %get-tuple-element.33), channel_id=1, source_target_pairs={{1,2},{2,1},{5,6},{6,5},{9,10},{10,9},{13,14},{14,13},{17,18},{18,... | collective-permute-start | bytes 393224 | tf_op jit(solution)/shard_map/ppermute | solution.py:335
  72.0 1.9 %collective-permute-start.3 = (f32[32,8,128]{2,1,0:T(8,128)S(1)}, f32[32,8,128]{2,1,0:T(8,128)S(1)}, u32[]{:S(2)}, u32[]{:S(2)}) collective-permute-start(f32[32,8,128]{2,1,0:T(8,128)S(1)} %get-tuple-element.35), channel_id=1, source_target_pairs={{0,1},{1,0},{2,3},{3,2},{4,5},{5,4},{6,7},{7,6},{8,9},{9,8},{10,11... | collective-permute-start | bytes 393224 | tf_op jit(solution)/shard_map/ppermute | solution.py:336
  73.9 0.9 %shard_map.106 = (f32[32,16,128]{2,1,0:T(8,128)S(1)}, f32[32,16,128]{2,1,0:T(8,128)}, f32[32,16,128]{2,1,0:T(8,128)}, f32[32,16,128]{2,1,0:T(8,128)}) custom-call(f32[32,16,128]{2,1,0:T(8,128)S(1)} %get-tuple-element.26.fx_ref, f32[32,16,128]{2,1,0:T(8,128)S(1)} %get-tuple-element.27.nd_ref, f32[32,16,128]{2,1,0:T(8,128)S(1)} %get-tuple-element.28.nm_ref, ...), custom_call_target="tpu_custom_call" | custom-call | tf_op jit(solution)/shard_map/pallas_call | solution.py:291
  74.8 0.0 collective-permute-done.2.far_ref
  74.8 0.4 collective-permute-done.3.near_ref
  75.2 1.1 %shard_map.107 = f32[32,16,128]{2,1,0:T(8,128)} custom-call(f32[32,8,128]{2,1,0:T(8,128)S(1)} %collective-permute-done.2.far_ref, f32[32,16,128]{2,1,0:T(8,128)S(1)} %get-tuple-element.34.own_ref, f32[32,8,128]{2,1,0:T(8,128)S(1)} %collective-permute-done.3.near_ref), custom_call_target="tpu_custom_call" | custom-call | tf_op jit(solution)/shard_map/pallas_call | solution.py:322
Async XLA Ops:
  1.3 26.4 %copy-start.2 = (f32[32,16,128]{2,1,0:T(8,128)S(1)}, f32[32,16,128]{2,1,0:T(8,128)}, u32[]{:S(2)}) copy-start(f32[32,16,128]{2,1,0:T(8,128)} %v_ref.3) | copy-start | bytes 786436
  3.0 24.7 %copy-start = (f32[32,16,128]{2,1,0:T(8,128)S(1)}, f32[32,16,128]{2,1,0:T(8,128)}, u32[]{:S(2)}) copy-start(f32[32,16,128]{2,1,0:T(8,128)} %d_ref.3) | copy-start | bytes 786436
  3.0 24.6 %copy-start.1 = (f32[32,16,128]{2,1,0:T(8,128)S(1)}, f32[32,16,128]{2,1,0:T(8,128)}, u32[]{:S(2)}) copy-start(f32[32,16,128]{2,1,0:T(8,128)} %m_ref.3) | copy-start | bytes 786436
  27.8 12.5 %copy-start.3 = (bf16[1152,128]{1,0:T(8,128)(2,1)S(1)}, bf16[1152,128]{1,0:T(8,128)(2,1)}, u32[]{:S(2)}) copy-start(bf16[1152,128]{1,0:T(8,128)(2,1)} %constant.6.taps_ref) | copy-start | bytes 884740
  41.6 22.7 %all-to-all-start.2 = ((f32[32,24,128]{2,1,0:T(8,128)}), f32[32,24,128]{2,1,0:T(8,128)S(1)}, u32[]{:S(2)}, u32[]{:S(2)}) async-start(f32[32,24,128]{2,1,0:T(8,128)} %shard_map.104), calls=%async_computation.2 | async-start | bytes 786432 | tf_op jit(solution)/shard_map/all_to_all | solution.py:340
  50.6 6.8 %collective-permute-start = (f32[3,8,16,128]{3,2,1,0:T(8,128)S(1)}, f32[3,8,16,128]{3,2,1,0:T(8,128)S(1)}, u32[]{:S(2)}, u32[]{:S(2)}) collective-permute-start(f32[3,8,16,128]{3,2,1,0:T(8,128)S(1)} %get-tuple-element.24), channel_id=1, source_target_pairs={{0,4},{4,0},{8,12},{12,8},{1,5},{5,1},{9,13},{13,9},{2,6},{6,2},{1... | collective-permute-start | bytes 589832 | tf_op jit(solution)/shard_map/ppermute | solution.py:336
  53.0 4.4 %collective-permute-start.1 = (f32[3,8,16,128]{3,2,1,0:T(8,128)S(1)}, f32[3,8,16,128]{3,2,1,0:T(8,128)S(1)}, u32[]{:S(2)}, u32[]{:S(2)}) collective-permute-start(f32[3,8,16,128]{3,2,1,0:T(8,128)S(1)} %get-tuple-element.25), channel_id=1, source_target_pairs={{4,8},{8,4},{5,9},{9,5},{6,10},{10,6},{7,11},{11,7},{20,24},{24,20... | collective-permute-start | bytes 589832 | tf_op jit(solution)/shard_map/ppermute | solution.py:335
  65.1 9.8 %collective-permute-start.2 = (f32[32,8,128]{2,1,0:T(8,128)S(1)}, f32[32,8,128]{2,1,0:T(8,128)S(1)}, u32[]{:S(2)}, u32[]{:S(2)}) collective-permute-start(f32[32,8,128]{2,1,0:T(8,128)S(1)} %get-tuple-element.33), channel_id=1, source_target_pairs={{1,2},{2,1},{5,6},{6,5},{9,10},{10,9},{13,14},{14,13},{17,18},{18,... | collective-permute-start | bytes 393224 | tf_op jit(solution)/shard_map/ppermute | solution.py:335
  72.0 3.2 %collective-permute-start.3 = (f32[32,8,128]{2,1,0:T(8,128)S(1)}, f32[32,8,128]{2,1,0:T(8,128)S(1)}, u32[]{:S(2)}, u32[]{:S(2)}) collective-permute-start(f32[32,8,128]{2,1,0:T(8,128)S(1)} %get-tuple-element.35), channel_id=1, source_target_pairs={{0,1},{1,0},{2,3},{3,2},{4,5},{5,4},{6,7},{7,6},{8,9},{9,8},{10,11... | collective-permute-start | bytes 393224 | tf_op jit(solution)/shard_map/ppermute | solution.py:336
